TPU v7x, 128 devices: a whole 4x4x4 slice. The times are simulated.
128 devices in a mesh: group: 8 (over z, core), patch: 16 (over y, x).
Axes of the slice: x: 4, y: 4, z: 4, core: 2. Of those that a mesh axis runs over, the one named last changes fastest.
Arguments:
- volume: float32 [4096, 8, 1024], P(('group', 'patch')), may hold values from 0.02 to 18, as said below
- block_place: int32 [4096], P(('group', 'patch')), may hold values from 0 to 4095, as said below
- measured: float32 [2, 512, 384], P(None, 'patch'), may hold values from 0.5 to 5.5
- live_rays: int32 [2, 512], replicated, may hold values from 24 to 48
Outputs:
- final_volume: float32 [4096, 8, 1024], P(('group', 'patch'))
- last_residual: float32 [8, 64, 384], P('group', 'patch')
Inputs may be any that keep to these rules, and one draw needn't show every extreme that they name: block_place lists the block positions of the 64 x 64 grid in the order of a Hilbert curve over that grid, begun at a drawn point of the curve (continuing from its end to its start) and turned or mirrored by one of the grid's eight symmetries; each position appears once. `volume`: positive.
All inputs are finite; a program needn't handle non-finite values.
Results may differ from a plain program's by a relative error of at most 0.0007.
Values may be sent and summed in bfloat16 or wider, within the bound.
No kernel may reach another device: no remote copies, remote signals or barrier semaphores. Data moves between devices by JAX's collectives and lax.ppermute only.
A program may use at most 128 MiB of HBM per device.

v0:
```python
import functools
import math

import jax
import jax.numpy as jnp
import numpy as np
from jax import lax
from jax.experimental import pallas as pl
from jax.experimental.pallas import tpu as pltpu
from jax.sharding import PartitionSpec as P

IMG_BLK = 64
BLK_SIDE = 32
VOX = BLK_SIDE * BLK_SIDE
RAYS_TILE = 48
NTILE = 64
ANG_SUB = 8
SUBSETS = 2
NSL = 8
SPREAD = 1.5
RELAX = 0.9
RAYS = NTILE * RAYS_TILE
WIN = 48
KALL = ANG_SUB * WIN
HALF_IMG = IMG_BLK * BLK_SIDE * 0.5
CHUNKS = 16
LOCAL = 32
LEAD = 23.75


def angle_consts(subset):
    out = []
    for a in range(ANG_SUB):
        theta = np.float32(math.pi * (a * SUBSETS + subset) / (ANG_SUB * SUBSETS))
        out.append((float(np.cos(theta)), float(np.sin(theta))))
    return out


def touched(cos, sin, ray0, chunk):
    v = np.arange(chunk * 128, chunk * 128 + 128)
    along = (v % BLK_SIDE - 15.5) * cos + (v // BLK_SIDE - 15.5) * sin
    low = along.min() + LEAD - 0.5 - SPREAD - 0.01
    high = along.max() + LEAD + 0.5 + SPREAD + 0.01
    return ray0 <= high and ray0 + 7 >= low


def place_of(place_ref, b, cos, sin):
    q = place_ref[b]
    x = ((q & (IMG_BLK - 1)) * BLK_SIDE).astype(jnp.float32) + (BLK_SIDE * 0.5 - HALF_IMG)
    y = ((q >> 6) * BLK_SIDE).astype(jnp.float32) + (BLK_SIDE * 0.5 - HALF_IMG)
    centre = x * cos + y * sin
    first = (centre + (RAYS * 0.5 - LEAD)).astype(jnp.int32)
    beta = centre + (RAYS * 0.5 - 0.5) - first.astype(jnp.float32)
    return first, beta


def fill_offsets(l_ref, subset):
    lane = lax.broadcasted_iota(jnp.int32, (8, 128), 1)
    for a, (cos, sin) in enumerate(angle_consts(subset)):
        for c in range(8):
            v = lane + c * 128
            dx = (v & 31).astype(jnp.float32) - 15.5
            dy = (v >> 5).astype(jnp.float32) - 15.5
            l_ref[a * 8 + c] = (dx * cos + dy * sin) * (1.0 / SPREAD)


def make_footprint(f_ref, l_ref, place_ref, b, subset):
    sub = lax.broadcasted_iota(jnp.int32, (8, 128), 0).astype(jnp.float32) * (1.0 / SPREAD)
    zero = jnp.zeros((8, 128), jnp.float32)
    firsts = []
    for a, (cos, sin) in enumerate(angle_consts(subset)):
        first, beta = place_of(place_ref, b, cos, sin)
        firsts.append(first)
        beta = beta * (1.0 / SPREAD)
        rays = [sub + (8 * r / SPREAD - beta) for r in range(WIN // 8)]
        for c in range(8):
            offs = l_ref[a * 8 + c]
            for t in range(WIN // 16):
                halves = []
                for r in (2 * t, 2 * t + 1):
                    if touched(cos, sin, 8 * r, c):
                        d = offs - rays[r]
                        m = jnp.maximum(1.0 - d * d, 0.0)
                        halves.append(m * m)
                    else:
                        halves.append(None)
                if halves[0] is None and halves[1] is None:
                    continue
                tile = jnp.concatenate([zero if h is None else h for h in halves], axis=0)
                f_ref[pl.ds(a * WIN + 16 * t, 16), pl.ds(c * 128, 128)] = tile.astype(jnp.bfloat16)
    return firsts


def zero_fill(f_ref):
    for r in range(KALL // 16):
        f_ref[pl.ds(16 * r, 16), :] = jnp.zeros((16, VOX), jnp.bfloat16)


def lanes(rows=8):
    return lax.broadcasted_iota(jnp.int32, (rows, 128), 1)


def project(x, f_ref):
    row = lax.broadcasted_iota(jnp.int32, (8, VOX), 0)
    ones = jnp.where(row == 0, 1.0, 0.0)
    both = jnp.concatenate([x, ones], axis=0).astype(jnp.bfloat16)
    return lax.dot_general(
        both, f_ref[...], (((1,), (1,)), ((), ())), preferred_element_type=jnp.float32
    )


def scatter_windows(acc_ref, contrib, firsts):
    lane = lanes(16)
    for a in range(ANG_SUB):
        at = a * WIN
        t0, lo = at // 128, at % 128
        piece = contrib[:, t0 * 128 : t0 * 128 + 128]
        if lo + WIN > 128:
            after = contrib[:, t0 * 128 + 128 : t0 * 128 + 256]
            piece = jnp.where(lane >= lo, piece, jnp.where(lane < lo + WIN - 128, after, 0.0))
        else:
            piece = jnp.where((lane >= lo) & (lane < lo + WIN), piece, 0.0)
        first = firsts[a]
        r = first & 127
        base = pl.multiple_of(first - r, 128)
        turned = pltpu.roll(piece, (r - lo + 128) & 127, 1)
        acc_ref[a, :, pl.ds(base, 128)] += jnp.where(lane >= r, turned, 0.0)
        acc_ref[a, :, pl.ds(base + 128, 128)] += jnp.where(lane < r, turned, 0.0)


def gather_windows(res_ref, firsts):
    lane = lanes(8)
    tiles = [jnp.zeros((8, 128), jnp.float32) for _ in range(KALL // 128)]
    for a in range(ANG_SUB):
        at = a * WIN
        t0, lo = at // 128, at % 128
        first = firsts[a]
        r = first & 127
        base = pl.multiple_of(first - r, 128)
        here = res_ref[a, :, pl.ds(base, 128)]
        after = res_ref[a, :, pl.ds(base + 128, 128)]
        turned = pltpu.roll(jnp.where(lane >= r, here, after), (lo - r + 128) & 127, 1)
        if lo + WIN > 128:
            tiles[t0] = jnp.where(lane >= lo, turned, tiles[t0])
            tiles[t0 + 1] = jnp.where(lane < lo + WIN - 128, turned, tiles[t0 + 1])
        else:
            tiles[t0] = jnp.where((lane >= lo) & (lane < lo + WIN), turned, tiles[t0])
    whole = jnp.concatenate(tiles, axis=1)
    row = lax.broadcasted_iota(jnp.int32, (8, KALL), 0)
    return jnp.concatenate([whole, jnp.where(row == 0, 1.0, 0.0)], axis=0).astype(jnp.bfloat16)


def chunk_at(a, c):
    return (c % 8) * 16 + a * 2 + c // 8


def write_chunks(out_ref, acc_ref):
    lane4 = lanes(4)
    for a in range(ANG_SUB):
        for m in range(CHUNKS // 2):
            for odd in range(2):
                whole = acc_ref[a, :, pl.ds((3 * m + 2 * odd) * 128, 128)]
                half = acc_ref[a, :, pl.ds((3 * m + 1) * 128, 128)]
                turned = pltpu.roll(half, 64, 1)
                if odd:
                    half, turned = turned, half
                packed = jnp.where(lane4 < 64, half[0:4], turned[4:8])
                sums = jnp.where(lanes(1) < 64, half[8:9], turned[8:9])
                d = chunk_at(a, 2 * m + odd)
                out_ref[d, 0:8, :] = whole[0:8]
                out_ref[d, 8:12, :] = packed
                out_ref[d, 12:13, :] = whole[8:9]
                out_ref[d, 13:14, :] = sums
                out_ref[d, 14:16, :] = jnp.zeros((2, 128), jnp.float32)


def read_chunks(res_ref, got_ref):
    lane = lanes(8)
    for a in range(ANG_SUB):
        for m in range(CHUNKS // 2):
            even = got_ref[chunk_at(a, 2 * m)].astype(jnp.float32)
            odd = got_ref[chunk_at(a, 2 * m + 1)].astype(jnp.float32)
            res_ref[a, :, pl.ds(3 * m * 128, 128)] = even[0:8]
            res_ref[a, :, pl.ds((3 * m + 2) * 128, 128)] = odd[0:8]
            he = jnp.concatenate([even[8:12], pltpu.roll(even[8:16], 64, 1)[0:4]], axis=0)
            ho = jnp.concatenate([pltpu.roll(odd[8:16], 64, 1)[0:4], odd[8:12]], axis=0)
            res_ref[a, :, pl.ds((3 * m + 1) * 128, 128)] = jnp.where(lane < 64, he, ho)
        res_ref[a, :, pl.ds(RAYS, 128)] = jnp.zeros((8, 128), jnp.float32)


def first_kernel(place_ref, x_ref, out_ref, f0, f1, l_ref, acc_ref):
    fill_offsets(l_ref, 0)
    zero_fill(f0)
    zero_fill(f1)
    acc_ref[...] = jnp.zeros_like(acc_ref)

    def step(i, carry):
        for k, f in enumerate((f0, f1)):
            b = 2 * i + k
            firsts = make_footprint(f, l_ref, place_ref, b, 0)
            scatter_windows(acc_ref, project(x_ref[b], f), firsts)
        return carry

    lax.fori_loop(0, LOCAL // 2, step, 0)
    write_chunks(out_ref, acc_ref)


def updated(x, total):
    return jnp.maximum(x + total[0:8] * (RELAX / total[8:9]), 0.0)


def middle_kernel(place_ref, got_ref, x_ref, new_ref, out_ref, f0, f1, l0, l1, acc_ref, res_ref):
    fill_offsets(l0, 0)
    fill_offsets(l1, 1)
    zero_fill(f0)
    zero_fill(f1)
    read_chunks(res_ref, got_ref)
    acc_ref[...] = jnp.zeros_like(acc_ref)

    def step(b, carry):
        firsts = make_footprint(f0, l0, place_ref, b, 0)
        total = jnp.dot(gather_windows(res_ref, firsts), f0[...], preferred_element_type=jnp.float32)
        x = updated(x_ref[b], total)
        new_ref[b] = x
        firsts = make_footprint(f1, l1, place_ref, b, 1)
        scatter_windows(acc_ref, project(x, f1), firsts)
        return carry

    lax.fori_loop(0, LOCAL, step, 0)
    write_chunks(out_ref, acc_ref)


def last_kernel(place_ref, got_ref, x_ref, new_ref, f0, f1, l_ref, res_ref):
    fill_offsets(l_ref, 1)
    zero_fill(f0)
    zero_fill(f1)
    read_chunks(res_ref, got_ref)

    def step(i, carry):
        for k, f in enumerate((f0, f1)):
            b = 2 * i + k
            firsts = make_footprint(f, l_ref, place_ref, b, 1)
            total = jnp.dot(
                gather_windows(res_ref, firsts), f[...], preferred_element_type=jnp.float32
            )
            new_ref[b] = updated(x_ref[b], total)
        return carry

    lax.fori_loop(0, LOCAL // 2, step, 0)


def residual_kernel(got_ref, meas_ref, live_ref, res_ref, send_ref):
    count = got_ref.shape[0]

    def add(i, totals):
        return tuple(t + got_ref[4 * i + k] for k, t in enumerate(totals))

    zero = jnp.zeros((16, 128), jnp.float32)
    parts = lax.fori_loop(0, count // 4, add, (zero,) * 4, unroll=4)
    total = (parts[0] + parts[1]) + (parts[2] + parts[3])
    row = lax.broadcasted_iota(jnp.int32, (16, 128), 0)
    sums = jnp.where(row < 8, total[12:13], total[13:14])
    differ = (meas_ref[...] - total / jnp.maximum(sums, 1.0)) * live_ref[...]
    res_ref[...] = differ
    rounded = differ.astype(jnp.bfloat16)

    def put(i, carry):
        send_ref[i] = rounded
        return carry

    lax.fori_loop(0, count, put, 0, unroll=8)


VM = pl.BlockSpec(memory_space=pltpu.VMEM)
SM = pl.BlockSpec(memory_space=pltpu.SMEM)
F_BUF = pltpu.VMEM((KALL, VOX), jnp.bfloat16)
L_BUF = pltpu.VMEM((ANG_SUB * 8, 8, 128), jnp.float32)
ACC_BUF = pltpu.VMEM((ANG_SUB, 16, RAYS + 128), jnp.float32)
RES_BUF = pltpu.VMEM((ANG_SUB, 8, RAYS + 128), jnp.float32)
PARAMS = pltpu.CompilerParams(vmem_limit_bytes=48 * 1024 * 1024)


def shape(dims, dtype=jnp.float32):
    return jax.ShapeDtypeStruct(dims, dtype)


def packed_rays(x, odd):
    whole = jnp.where(odd, x[:, 64:192], x[:, 0:128])
    half = jnp.where(odd, x[:, 0:64], x[:, 128:192])
    return jnp.concatenate(
        [whole, jnp.concatenate([half[0:4], half[4:8]], axis=1), jnp.zeros((4, 128), x.dtype)], axis=0
    )


def unpacked_rays(chunk, odd):
    whole = chunk[0:8]
    half = jnp.concatenate([chunk[8:12, 0:64], chunk[8:12, 64:128]], axis=0)
    return jnp.where(
        odd, jnp.concatenate([half, whole], axis=1), jnp.concatenate([whole, half], axis=1)
    )


def shards(volume, block_place, measured, live_rays):
    axes = ("group", "patch")
    group = lax.axis_index("group")
    patch = lax.axis_index("patch")
    count = lax.axis_size("group") * lax.axis_size("patch")
    odd = group % 2 == 1
    own = ANG_SUB * NTILE // count

    def masks(subset):
        rows = lax.dynamic_slice_in_dim(measured[subset], group * own, own, 0)
        rows = rows.reshape(own * RAYS_TILE, NSL).T
        live = lax.dynamic_slice_in_dim(
            live_rays[subset], (patch * lax.axis_size("group") + group) * own, own, 0
        )
        live = (jnp.arange(RAYS_TILE, dtype=jnp.int32)[None, :] < live[:, None]).astype(jnp.float32)
        live = jnp.broadcast_to(live.reshape(1, -1), (NSL, own * RAYS_TILE))
        return packed_rays(rows, odd), packed_rays(live, odd)

    def exchanged(sent):
        return lax.all_to_all(sent, axes, 0, 0, tiled=True)

    def residual(sent, subset):
        meas, live = masks(subset)
        return pl.pallas_call(
            residual_kernel,
            out_shape=(shape((16, 128)), shape((count, 16, 128), jnp.bfloat16)),
            in_specs=[VM] * 3,
            out_specs=(VM, VM),
            compiler_params=PARAMS,
        )(exchanged(sent), meas, live)

    sent = pl.pallas_call(
        first_kernel,
        out_shape=shape((count, 16, 128)),
        in_specs=[SM, VM],
        out_specs=VM,
        scratch_shapes=[F_BUF, F_BUF, L_BUF, ACC_BUF],
        compiler_params=PARAMS,
    )(block_place, volume)
    _, rounded = residual(sent, 0)
    estimate, sent = pl.pallas_call(
        middle_kernel,
        out_shape=(shape(volume.shape), shape((count, 16, 128))),
        in_specs=[SM, VM, VM],
        out_specs=(VM, VM),
        scratch_shapes=[F_BUF, F_BUF, L_BUF, L_BUF, ACC_BUF, RES_BUF],
        compiler_params=PARAMS,
    )(block_place, exchanged(rounded), volume)
    last, rounded = residual(sent, 1)
    final = pl.pallas_call(
        last_kernel,
        out_shape=shape(volume.shape),
        in_specs=[SM, VM, VM],
        out_specs=VM,
        scratch_shapes=[F_BUF, F_BUF, L_BUF, RES_BUF],
        compiler_params=PARAMS,
    )(block_place, exchanged(rounded), estimate)
    last = unpacked_rays(last, odd).T.reshape(1, own, RAYS_TILE * NSL)
    return final, last


def solution(mesh):
    return jax.shard_map(
        shards,
        mesh=mesh,
        in_specs=(
            P(("group", "patch"), None, None),
            P(("group", "patch")),
            P(None, "patch", None),
            P(),
        ),
        out_specs=(P(("group", "patch"), None, None), P("group", "patch", None)),
        check_vma=False,
    )
```

profile of v0, /device:TPU:1, one launch (start us, length us, event | category | flops | bytes accessed | tf_op | source)
XLA Modules:
  0.0 159.0 jit_solution(9228670191677789887)
XLA Ops:
  0.6 1.2 copy-done
  1.9 0.7 copy-done.2
  2.5 17.2 %shard_map.59 = f32[128,16,128]{2,1,0:T(8,128)} custom-call(s32[32]{0:T(128)S(1)} %copy-done.2, f32[32,8,1024]{2,1,0:T(8,128)S(1)} %copy-done), custom_call_target="tpu_custom_call" | custom-call | tf_op jit(solution)/shard_map/pallas_call | solution.py:334
  19.7 11.5 %all-to-all-start = ((f32[128,16,128]{2,1,0:T(8,128)}), f32[128,16,128]{2,1,0:T(8,128)S(1)}, u32[]{:S(2)}, u32[]{:S(2)}) async-start(f32[128,16,128]{2,1,0:T(8,128)} %shard_map.59), calls=%async_computation | async-start | bytes 2097152 | tf_op jit(solution)/shard_map/all_to_all | solution.py:322
  31.3 0.7 copy-done.5
  31.9 0.1 fusion.8
  32.0 0.1 fusion.7
  32.1 0.1 fusion.1
  32.1 0.1 reshape.98
  32.2 0.1 fusion.2
  32.3 0.1 reshape.99
  32.4 0.1 reshape.95
  32.6 0.1 copy.6
  32.6 0.1 reshape.96
  32.7 0.1 copy.7
  32.8 0.1 pad.21.clone
  32.9 0.1 fusion.3
  33.0 0.1 slice_select_fusion.1
  33.1 0.1 maximum_maximum_fusion.3
  33.2 16.8 %all-to-all-done.got_ref = f32[128,16,128]{2,1,0:T(8,128)S(1)} async-done(((f32[128,16,128]{2,1,0:T(8,128)}), f32[128,16,128]{2,1,0:T(8,128)S(1)}, u32[]{:S(2)}, u32[]{:S(2)}) %all-to-all-start) | async-done | bytes 1048608 | tf_op jit(solution)/shard_map/all_to_all | solution.py:322
  50.0 0.8 shard_map.60
  50.8 18.3 %all_to_all.20.got_ref = bf16[128,16,128]{2,1,0:T(8,128)(2,1)S(1)} all-to-all(bf16[128,16,128]{2,1,0:T(8,128)(2,1)S(1)} %get-tuple-element.7), channel_id=1, replica_groups=mesh['group'=8,'patch'=16] {'group','patch'}, dimensions={0} | all-to-all | bytes 1048576 | tf_op jit(solution)/shard_map/all_to_all | solution.py:322
  69.1 32.1 %shard_map.61 = (f32[32,8,1024]{2,1,0:T(8,128)S(1)}, f32[128,16,128]{2,1,0:T(8,128)S(1)}) custom-call(s32[32]{0:T(128)S(1)} %copy-done.3, bf16[128,16,128]{2,1,0:T(8,128)(2,1)S(1)} %all_to_all.20.got_ref, f32[32,8,1024]{2,1,0:T(8,128)S(1)} %copy-done.1), custom_call_target="tpu_custom_call" | custom-call | tf_op jit(solution)/shard_map/pallas_call | solution.py:343
  101.2 22.8 %all_to_all.21.got_ref = f32[128,16,128]{2,1,0:T(8,128)S(1)} all-to-all(f32[128,16,128]{2,1,0:T(8,128)S(1)} %get-tuple-element.8), channel_id=1, replica_groups=mesh['group'=8,'patch'=16] {'group','patch'}, dimensions={0} | all-to-all | bytes 2097152 | tf_op jit(solution)/shard_map/all_to_all | solution.py:322
  124.0 1.0 shard_map.62
  125.0 4.7 %all-to-all-start.3 = ((bf16[128,16,128]{2,1,0:T(8,128)(2,1)}), bf16[128,16,128]{2,1,0:T(8,128)(2,1)S(1)}, u32[]{:S(2)}, u32[]{:S(2)}) async-start(bf16[128,16,128]{2,1,0:T(8,128)(2,1)} %get-tuple-element.9), calls=%async_computation.3 | async-start | bytes 1048576 | tf_op jit(solution)/shard_map/all_to_all | solution.py:322
  129.7 0.1 fusion.10
  129.8 0.1 fusion
  129.9 0.1 copy.8
  130.0 0.7 reshape.97
  130.7 13.1 %all-to-all-done.3.got_ref = bf16[128,16,128]{2,1,0:T(8,128)(2,1)S(1)} async-done(((bf16[128,16,128]{2,1,0:T(8,128)(2,1)}), bf16[128,16,128]{2,1,0:T(8,128)(2,1)S(1)}, u32[]{:S(2)}, u32[]{:S(2)}) %all-to-all-start.3) | async-done | bytes 524320 | tf_op jit(solution)/shard_map/all_to_all | solution.py:322
  143.8 15.3 %shard_map.63 = f32[32,8,1024]{2,1,0:T(8,128)} custom-call(s32[32]{0:T(128)S(1)} %copy-done.3, bf16[128,16,128]{2,1,0:T(8,128)(2,1)S(1)} %all-to-all-done.3.got_ref, f32[32,8,1024]{2,1,0:T(8,128)S(1)} %get-tuple-element.10.x_ref), custom_call_target="tpu_custom_call" | custom-call | tf_op jit(solution)/shard_map/pallas_call | solution.py:352
  (23 shorter events, 0.1 us)
Async XLA Ops:
  0.6 1.2 copy-start
  1.9 0.7 copy-start.2
  19.7 12.7 %copy-start.4 = (f32[2,32,384]{2,1,0:T(8,128)S(1)}, f32[2,32,384]{2,1,0:T(8,128)}, u32[]{:S(2)}) copy-start(f32[2,32,384]{2,1,0:T(8,128)} %param.6) | copy-start | bytes 294916
  19.7 30.3 %all-to-all-start = ((f32[128,16,128]{2,1,0:T(8,128)}), f32[128,16,128]{2,1,0:T(8,128)S(1)}, u32[]{:S(2)}, u32[]{:S(2)}) async-start(f32[128,16,128]{2,1,0:T(8,128)} %shard_map.59), calls=%async_computation | async-start | bytes 2097152 | tf_op jit(solution)/shard_map/all_to_all | solution.py:322
  31.2 0.7 copy-start.5
  50.0 19.0 %copy-start.1 = (f32[32,8,1024]{2,1,0:T(8,128)S(1)}, f32[32,8,1024]{2,1,0:T(8,128)}, u32[]{:S(2)}) copy-start(f32[32,8,1024]{2,1,0:T(8,128)} %x_ref.3) | copy-start | bytes 3145732
  50.8 18.3 %copy-start.3 = (s32[32]{0:T(128)S(1)}, s32[32]{0:T(128)}, u32[]{:S(2)}) copy-start(s32[32]{0:T(128)} %place_ref.5) | copy-start | bytes 388
  125.0 18.8 %all-to-all-start.3 = ((bf16[128,16,128]{2,1,0:T(8,128)(2,1)}), bf16[128,16,128]{2,1,0:T(8,128)(2,1)S(1)}, u32[]{:S(2)}, u32[]{:S(2)}) async-start(bf16[128,16,128]{2,1,0:T(8,128)(2,1)} %get-tuple-element.9), calls=%async_computation.3 | async-start | bytes 1048576 | tf_op jit(solution)/shard_map/all_to_all | solution.py:322
where the time goes:
time: 159 us
  Pallas kernels  66.3 us (42%)
  blocking collectives  41 us (26%)
  waiting for transfers between devices  29.9 us (19%)
  starting transfers between devices  16.2 us (10%)
  local copies, waits for them, and re-layouts  4.23 us (3%)
    all_to_all x2, blocking collectives, exchanged(): return lax.all_to_all(sent, axes, 0, 0, tiled=True)  41 us
    pallas_call x1, Pallas kernels, shards(): pl.pallas_call(middle_kernel, out_shape=(shape(volume.shape), shape((coun...  32.1 us
    all_to_all x2, waiting for transfers between devices, exchanged(): return lax.all_to_all(sent, axes, 0, 0, tiled=True)  29.9 us
    pallas_call x1, Pallas kernels, shards(): pl.pallas_call(first_kernel, out_shape=shape((count, 16, 128)), in_specs=...  17.2 us
    all_to_all x2, starting transfers between devices, exchanged(): return lax.all_to_all(sent, axes, 0, 0, tiled=True)  16.2 us
    pallas_call x1, Pallas kernels, shards(): pl.pallas_call(last_kernel, out_shape=shape(volume.shape), in_specs=[SM,...  15.3 us
  transfers between devices with their start and end apart: 2, of which 2 were waited for; matrix products, arithmetic and copies ran while one was open for 1% of the time, Pallas kernels for 0%

commit v1 on v0

--- a/solution.py
+++ b/solution.py
@@ -25,6 +25,8 @@
 HALF_IMG = IMG_BLK * BLK_SIDE * 0.5
 CHUNKS = 16
 LOCAL = 32
+DEPTH = 12
+TOGETHER = 4
 LEAD = 23.75
 
 
@@ -64,16 +66,17 @@
             l_ref[a * 8 + c] = (dx * cos + dy * sin) * (1.0 / SPREAD)
 
 
-def make_footprint(f_ref, l_ref, place_ref, b, subset):
+def windows(place_ref, b, subset):
+    return [place_of(place_ref, b, cos, sin) for cos, sin in angle_consts(subset)]
+
+
+def make_footprint(f_ref, l_ref, at, subset, part):
     sub = lax.broadcasted_iota(jnp.int32, (8, 128), 0).astype(jnp.float32) * (1.0 / SPREAD)
     zero = jnp.zeros((8, 128), jnp.float32)
-    firsts = []
     for a, (cos, sin) in enumerate(angle_consts(subset)):
-        first, beta = place_of(place_ref, b, cos, sin)
-        firsts.append(first)
-        beta = beta * (1.0 / SPREAD)
+        beta = at[a][1] * (1.0 / SPREAD)
         rays = [sub + (8 * r / SPREAD - beta) for r in range(WIN // 8)]
-        for c in range(8):
+        for c in (2 * part, 2 * part + 1):
             offs = l_ref[a * 8 + c]
             for t in range(WIN // 16):
                 halves = []
@@ -88,7 +91,6 @@
                     continue
                 tile = jnp.concatenate([zero if h is None else h for h in halves], axis=0)
                 f_ref[pl.ds(a * WIN + 16 * t, 16), pl.ds(c * 128, 128)] = tile.astype(jnp.bfloat16)
-    return firsts
 
 
 def zero_fill(f_ref):
@@ -100,27 +102,28 @@
     return lax.broadcasted_iota(jnp.int32, (rows, 128), 1)
 
 
-def project(x, f_ref):
-    row = lax.broadcasted_iota(jnp.int32, (8, VOX), 0)
-    ones = jnp.where(row == 0, 1.0, 0.0)
-    both = jnp.concatenate([x, ones], axis=0).astype(jnp.bfloat16)
+def with_ones(x):
+    row = lax.broadcasted_iota(jnp.int32, x.shape, 0)
+    return jnp.concatenate([x, jnp.where(row == 0, 1.0, 0.0)], axis=0).astype(jnp.bfloat16)
+
+
+def project(x, f_ref, cols=slice(None)):
     return lax.dot_general(
-        both, f_ref[...], (((1,), (1,)), ((), ())), preferred_element_type=jnp.float32
+        x[:, cols], f_ref[:, cols], (((1,), (1,)), ((), ())), preferred_element_type=jnp.float32
     )
 
 
-def scatter_windows(acc_ref, contrib, firsts):
+def scatter_windows(acc_ref, contrib, at):
     lane = lanes(16)
     for a in range(ANG_SUB):
-        at = a * WIN
-        t0, lo = at // 128, at % 128
+        t0, lo = a * WIN // 128, a * WIN % 128
         piece = contrib[:, t0 * 128 : t0 * 128 + 128]
         if lo + WIN > 128:
             after = contrib[:, t0 * 128 + 128 : t0 * 128 + 256]
             piece = jnp.where(lane >= lo, piece, jnp.where(lane < lo + WIN - 128, after, 0.0))
         else:
             piece = jnp.where((lane >= lo) & (lane < lo + WIN), piece, 0.0)
-        first = firsts[a]
+        first = at[a][0]
         r = first & 127
         base = pl.multiple_of(first - r, 128)
         turned = pltpu.roll(piece, (r - lo + 128) & 127, 1)
@@ -128,13 +131,12 @@
         acc_ref[a, :, pl.ds(base + 128, 128)] += jnp.where(lane < r, turned, 0.0)
 
 
-def gather_windows(res_ref, firsts):
+def gather_windows(res_ref, at):
     lane = lanes(8)
     tiles = [jnp.zeros((8, 128), jnp.float32) for _ in range(KALL // 128)]
     for a in range(ANG_SUB):
-        at = a * WIN
-        t0, lo = at // 128, at % 128
-        first = firsts[a]
+        t0, lo = a * WIN // 128, a * WIN % 128
+        first = at[a][0]
         r = first & 127
         base = pl.multiple_of(first - r, 128)
         here = res_ref[a, :, pl.ds(base, 128)]
@@ -145,9 +147,7 @@
             tiles[t0 + 1] = jnp.where(lane < lo + WIN - 128, turned, tiles[t0 + 1])
         else:
             tiles[t0] = jnp.where((lane >= lo) & (lane < lo + WIN), turned, tiles[t0])
-    whole = jnp.concatenate(tiles, axis=1)
-    row = lax.broadcasted_iota(jnp.int32, (8, KALL), 0)
-    return jnp.concatenate([whole, jnp.where(row == 0, 1.0, 0.0)], axis=0).astype(jnp.bfloat16)
+    return with_ones(jnp.concatenate(tiles, axis=1))
 
 
 def chunk_at(a, c):
@@ -188,20 +188,37 @@
         res_ref[a, :, pl.ds(RAYS, 128)] = jnp.zeros((8, 128), jnp.float32)
 
 
+def two_slots(step, f0, f1, make):
+    for part in range(4):
+        make(f0, 0)(part)
+
+    def both(i, carry):
+        step(2 * i, f0, make(f1, 2 * i + 1))
+        step(2 * i + 1, f1, make(f0, jnp.minimum(2 * i + 2, LOCAL - 1)))
+        return carry
+
+    lax.fori_loop(0, LOCAL // 2, both, 0)
+
+
 def first_kernel(place_ref, x_ref, out_ref, f0, f1, l_ref, acc_ref):
     fill_offsets(l_ref, 0)
     zero_fill(f0)
     zero_fill(f1)
     acc_ref[...] = jnp.zeros_like(acc_ref)
 
-    def step(i, carry):
-        for k, f in enumerate((f0, f1)):
-            b = 2 * i + k
-            firsts = make_footprint(f, l_ref, place_ref, b, 0)
-            scatter_windows(acc_ref, project(x_ref[b], f), firsts)
-        return carry
-
-    lax.fori_loop(0, LOCAL // 2, step, 0)
+    def make(f, b):
+        at = windows(place_ref, b, 0)
+        return lambda part: make_footprint(f, l_ref, at, 0, part)
+
+    def step(b, f, fill):
+        x = with_ones(x_ref[b])
+        contrib = 0.0
+        for part in range(4):
+            contrib = contrib + project(x, f, slice(part * 256, part * 256 + 256))
+            fill(part)
+        scatter_windows(acc_ref, contrib, windows(place_ref, b, 0))
+
+    two_slots(step, f0, f1, make)
     write_chunks(out_ref, acc_ref)
 
 
@@ -209,47 +226,97 @@
     return jnp.maximum(x + total[0:8] * (RELAX / total[8:9]), 0.0)
 
 
-def middle_kernel(place_ref, got_ref, x_ref, new_ref, out_ref, f0, f1, l0, l1, acc_ref, res_ref):
-    fill_offsets(l0, 0)
-    fill_offsets(l1, 1)
-    zero_fill(f0)
-    zero_fill(f1)
-    read_chunks(res_ref, got_ref)
-    acc_ref[...] = jnp.zeros_like(acc_ref)
+def footprint_kernel(subset, place_ref, out_ref, token_ref, slots, l_ref, sems):
+    depth = slots.shape[0]
+    token_ref[...] = jnp.zeros_like(token_ref)
+    fill_offsets(l_ref, subset)
+    for k in range(depth):
+        zero_fill(slots.at[k])
 
     def step(b, carry):
-        firsts = make_footprint(f0, l0, place_ref, b, 0)
-        total = jnp.dot(gather_windows(res_ref, firsts), f0[...], preferred_element_type=jnp.float32)
+        k = lax.rem(b, depth)
+
+        @pl.when(b >= depth)
+        def _():
+            pltpu.make_async_copy(slots.at[k], out_ref.at[b - depth], sems.at[k]).wait()
+
+        at = windows(place_ref, b, subset)
+        for part in range(4):
+            make_footprint(slots.at[k], l_ref, at, subset, part)
+        pltpu.make_async_copy(slots.at[k], out_ref.at[b], sems.at[k]).start()
+        return carry
+
+    lax.fori_loop(0, LOCAL, step, 0)
+    for k in range(depth):
+        b = LOCAL - depth + k
+        pltpu.make_async_copy(slots.at[b % depth], out_ref.at[b], sems.at[b % depth]).wait()
+
+
+def streamed(sources, slots, sems, before, step):
+    many = range(len(sources))
+
+    def copy(n, b):
+        k = lax.rem(b, DEPTH)
+        return pltpu.make_async_copy(sources[n].at[b], slots[n].at[k], sems.at[n, k])
+
+    for b in range(DEPTH - TOGETHER):
+        for n in many:
+            copy(n, b).start()
+    before()
+
+    def some(i, carry):
+        first = i * TOGETHER
+
+        @pl.when(first + DEPTH - TOGETHER < LOCAL)
+        def _():
+            for k in range(TOGETHER):
+                for n in many:
+                    copy(n, first + DEPTH - TOGETHER + k).start()
+
+        for k in range(TOGETHER):
+            for n in many:
+                copy(n, first + k).wait()
+        for k in range(TOGETHER):
+            b = first + k
+            step(b, [slots[n].at[lax.rem(b, DEPTH)] for n in many])
+        return carry
+
+    lax.fori_loop(0, LOCAL // TOGETHER, some, 0)
+
+
+def middle_kernel(
+    place_ref, got_ref, x_ref, fa, fb, new_ref, out_ref, a_slots, b_slots, acc_ref, res_ref, sems
+):
+    def before():
+        read_chunks(res_ref, got_ref)
+        acc_ref[...] = jnp.zeros_like(acc_ref)
+
+    def step(b, refs):
+        res = gather_windows(res_ref, windows(place_ref, b, 0))
+        total = jnp.dot(res, refs[0][...], preferred_element_type=jnp.float32)
         x = updated(x_ref[b], total)
         new_ref[b] = x
-        firsts = make_footprint(f1, l1, place_ref, b, 1)
-        scatter_windows(acc_ref, project(x, f1), firsts)
-        return carry
-
-    lax.fori_loop(0, LOCAL, step, 0)
+        x = with_ones(x)
+        scatter_windows(acc_ref, project(x, refs[1]), windows(place_ref, b, 1))
+
+    streamed((fa, fb), (a_slots, b_slots), sems, before, step)
     write_chunks(out_ref, acc_ref)
 
 
-def last_kernel(place_ref, got_ref, x_ref, new_ref, f0, f1, l_ref, res_ref):
-    fill_offsets(l_ref, 1)
-    zero_fill(f0)
-    zero_fill(f1)
-    read_chunks(res_ref, got_ref)
-
-    def step(i, carry):
-        for k, f in enumerate((f0, f1)):
-            b = 2 * i + k
-            firsts = make_footprint(f, l_ref, place_ref, b, 1)
-            total = jnp.dot(
-                gather_windows(res_ref, firsts), f[...], preferred_element_type=jnp.float32
-            )
-            new_ref[b] = updated(x_ref[b], total)
-        return carry
-
-    lax.fori_loop(0, LOCAL // 2, step, 0)
-
-
-def residual_kernel(got_ref, meas_ref, live_ref, res_ref, send_ref):
+def last_kernel(place_ref, got_ref, x_ref, fb, new_ref, slots, res_ref, sems):
+    def before():
+        read_chunks(res_ref, got_ref)
+
+    def step(b, refs):
+        res = gather_windows(res_ref, windows(place_ref, b, 1))
+        total = jnp.dot(res, refs[0][...], preferred_element_type=jnp.float32)
+        new_ref[b] = updated(x_ref[b], total)
+
+    streamed((fb,), (slots,), sems, before, step)
+
+
+def residual_kernel(got_ref, meas_ref, live_ref, *refs):
+    res_ref, send_ref = refs[-2:]
     count = got_ref.shape[0]
 
     def add(i, totals):
@@ -272,7 +339,9 @@
 
 
 VM = pl.BlockSpec(memory_space=pltpu.VMEM)
+ANY = pl.BlockSpec(memory_space=pl.ANY)
 SM = pl.BlockSpec(memory_space=pltpu.SMEM)
+F_RING = pltpu.VMEM((DEPTH, KALL, VOX), jnp.bfloat16)
 F_BUF = pltpu.VMEM((KALL, VOX), jnp.bfloat16)
 L_BUF = pltpu.VMEM((ANG_SUB * 8, 8, 128), jnp.float32)
 ACC_BUF = pltpu.VMEM((ANG_SUB, 16, RAYS + 128), jnp.float32)
@@ -321,15 +390,15 @@
     def exchanged(sent):
         return lax.all_to_all(sent, axes, 0, 0, tiled=True)
 
-    def residual(sent, subset):
+    def residual(sent, subset, *ready):
         meas, live = masks(subset)
         return pl.pallas_call(
             residual_kernel,
             out_shape=(shape((16, 128)), shape((count, 16, 128), jnp.bfloat16)),
-            in_specs=[VM] * 3,
+            in_specs=[VM] * (3 + len(ready)),
             out_specs=(VM, VM),
             compiler_params=PARAMS,
-        )(exchanged(sent), meas, live)
+        )(exchanged(sent), meas, live, *ready)
 
     sent = pl.pallas_call(
         first_kernel,
@@ -339,24 +408,39 @@
         scratch_shapes=[F_BUF, F_BUF, L_BUF, ACC_BUF],
         compiler_params=PARAMS,
     )(block_place, volume)
-    _, rounded = residual(sent, 0)
+    def footprints(subset):
+        return pl.pallas_call(
+            functools.partial(footprint_kernel, subset),
+            out_shape=(shape((LOCAL, KALL, VOX), jnp.bfloat16), shape((8, 128))),
+            in_specs=[SM],
+            out_specs=(ANY, VM),
+            scratch_shapes=[F_RING, L_BUF, pltpu.SemaphoreType.DMA((DEPTH,))],
+            compiler_params=PARAMS,
+            cost_estimate=pl.CostEstimate(
+                flops=0, bytes_accessed=LOCAL * KALL * VOX * 2, transcendentals=0
+            ),
+        )(block_place)
+
+    fa, token = footprints(0)
+    _, rounded = residual(sent, 0, token)
+    fb, _ = footprints(1)
     estimate, sent = pl.pallas_call(
         middle_kernel,
         out_shape=(shape(volume.shape), shape((count, 16, 128))),
-        in_specs=[SM, VM, VM],
+        in_specs=[SM, VM, VM, ANY, ANY],
         out_specs=(VM, VM),
-        scratch_shapes=[F_BUF, F_BUF, L_BUF, L_BUF, ACC_BUF, RES_BUF],
+        scratch_shapes=[F_RING, F_RING, ACC_BUF, RES_BUF, pltpu.SemaphoreType.DMA((2, DEPTH))],
         compiler_params=PARAMS,
-    )(block_place, exchanged(rounded), volume)
+    )(block_place, exchanged(rounded), volume, fa, fb)
     last, rounded = residual(sent, 1)
     final = pl.pallas_call(
         last_kernel,
         out_shape=shape(volume.shape),
-        in_specs=[SM, VM, VM],
+        in_specs=[SM, VM, VM, ANY],
         out_specs=VM,
-        scratch_shapes=[F_BUF, F_BUF, L_BUF, RES_BUF],
+        scratch_shapes=[F_RING, RES_BUF, pltpu.SemaphoreType.DMA((1, DEPTH))],
         compiler_params=PARAMS,
-    )(block_place, exchanged(rounded), estimate)
+    )(block_place, exchanged(rounded), estimate, fb)
     last = unpacked_rays(last, odd).T.reshape(1, own, RAYS_TILE * NSL)
     return final, last
 

time: 159 us -> 146 us (0.918)
  blocking collectives: 41 us -> 26.1 us
  waiting for transfers between devices: 29.9 us -> 20.4 us
  starting transfers between devices: 16.2 us -> 21 us
  local copies, waits for them, and re-layouts: 4.23 us -> 8.31 us
  Pallas kernels: 66.3 us -> 68.7 us
    pallas_call x0 -> x2, Pallas kernels: none -> 21.3 us  [footprints(): pl.pallas_call(functools.partial(footprint_kernel, subset), out_shape=(sh...]
    all_to_all x2 -> x1, blocking collectives: 41 us -> 26.1 us  [exchanged(): return lax.all_to_all(sent, axes, 0, 0, tiled=True)]
    pallas_call x1, Pallas kernels: 32.1 us -> 18.4 us  [shards(): pl.pallas_call(middle_kernel, out_shape=(shape(volume.shape), shape((coun...]
    all_to_all x2 -> x3, waiting for transfers between devices: 29.9 us -> 20.4 us  [exchanged(): return lax.all_to_all(sent, axes, 0, 0, tiled=True)]
    all_to_all x2 -> x3, starting transfers between devices: 16.2 us -> 21 us  [exchanged(): return lax.all_to_all(sent, axes, 0, 0, tiled=True)]
    pallas_call x1, Pallas kernels: 15.3 us -> 10.7 us  [shards(): pl.pallas_call(last_kernel, out_shape=shape(volume.shape), in_specs=[SM,...]
    unnamed x12 -> x14, local copies, waits for them, and re-layouts: 2.56 us -> 5.06 us
  transfers between devices with their start and end apart: 2 -> 3, of which waited for: 2 -> 3; matrix products, arithmetic and copies ran while one was open for 1% -> 3% of each run, Pallas kernels for 0% -> 15%
where the time goes in v1:
time: 146 us
  Pallas kernels  68.7 us (47%)
  blocking collectives  26.1 us (18%)
  starting transfers between devices  21 us (14%)
  waiting for transfers between devices  20.4 us (14%)
  local copies, waits for them, and re-layouts  8.31 us (6%)
    all_to_all x1, blocking collectives, exchanged(): return lax.all_to_all(sent, axes, 0, 0, tiled=True)  26.1 us
    pallas_call x2, Pallas kernels, footprints(): pl.pallas_call(functools.partial(footprint_kernel, subset), out_shape=(sh...  21.3 us
    all_to_all x3, starting transfers between devices, exchanged(): return lax.all_to_all(sent, axes, 0, 0, tiled=True)  21 us
    all_to_all x3, waiting for transfers between devices, exchanged(): return lax.all_to_all(sent, axes, 0, 0, tiled=True)  20.4 us
    pallas_call x1, Pallas kernels, shards(): pl.pallas_call(middle_kernel, out_shape=(shape(volume.shape), shape((coun...  18.4 us
    pallas_call x1, Pallas kernels, shards(): pl.pallas_call(first_kernel, out_shape=shape((count, 16, 128)), in_specs=...  16.4 us
    pallas_call x1, Pallas kernels, shards(): pl.pallas_call(last_kernel, out_shape=shape(volume.shape), in_specs=[SM,...  10.7 us
    unnamed x14, local copies, waits for them, and re-layouts  5.06 us
  transfers between devices with their start and end apart: 3, of which 3 were waited for; matrix products, arithmetic and copies ran while one was open for 3% of the time, Pallas kernels for 15%

profile of v1, /device:TPU:1, one launch (start us, length us, event | category | flops | bytes accessed | tf_op | source)
XLA Modules:
  0.0 145.8 jit_solution(6043123131331985413)
XLA Ops:
  0.6 1.2 copy-done
  1.9 0.7 copy-done.2
  2.5 16.4 %shard_map.59 = f32[128,16,128]{2,1,0:T(8,128)} custom-call(s32[32]{0:T(128)S(1)} %copy-done.2, f32[32,8,1024]{2,1,0:T(8,128)S(1)} %copy-done), custom_call_target="tpu_custom_call" | custom-call | tf_op jit(solution)/shard_map/pallas_call | solution.py:403
  18.9 11.5 %all-to-all-start = ((f32[128,16,128]{2,1,0:T(8,128)}), f32[128,16,128]{2,1,0:T(8,128)S(1)}, u32[]{:S(2)}, u32[]{:S(2)}) async-start(f32[128,16,128]{2,1,0:T(8,128)} %shard_map.59), calls=%async_computation | async-start | bytes 2097152 | tf_op jit(solution)/shard_map/all_to_all | solution.py:391
  30.5 0.6 copy-done.3
  31.1 10.3 %shard_map.60 = (bf16[32,384,1024]{2,1,0:T(8,128)(2,1)}, f32[8,128]{1,0:T(8,128)S(1)}) custom-call(s32[32]{0:T(128)S(1)} %copy-done.3), custom_call_target="tpu_custom_call" | custom-call | bytes 25165824 | tf_op jit(solution)/shard_map/pallas_call | solution.py:412
  41.4 0.8 fusion.11
  42.4 0.1 reshape.98
  42.6 0.1 reshape.99
  42.7 0.8 fusion.9
  43.5 0.1 reshape.95
  43.7 0.1 reshape.96
  43.9 0.1 pad.21.clone
  44.1 0.1 slice_select_fusion.1
  44.2 0.1 maximum_maximum_fusion.3
  44.3 5.0 %all-to-all-done.got_ref = f32[128,16,128]{2,1,0:T(8,128)S(1)} async-done(((f32[128,16,128]{2,1,0:T(8,128)}), f32[128,16,128]{2,1,0:T(8,128)S(1)}, u32[]{:S(2)}, u32[]{:S(2)}) %all-to-all-start) | async-done | bytes 1048608 | tf_op jit(solution)/shard_map/all_to_all | solution.py:391
  49.2 1.0 shard_map.61
  50.2 4.8 %all-to-all-start.1 = ((bf16[128,16,128]{2,1,0:T(8,128)(2,1)}), bf16[128,16,128]{2,1,0:T(8,128)(2,1)S(1)}, u32[]{:S(2)}, u32[]{:S(2)}) async-start(bf16[128,16,128]{2,1,0:T(8,128)(2,1)} %get-tuple-element.11), calls=%async_computation.1 | async-start | bytes 1048576 | tf_op jit(solution)/shard_map/all_to_all | solution.py:391
  55.0 0.6 copy-done.4
  55.7 11.0 %shard_map.62 = (bf16[32,384,1024]{2,1,0:T(8,128)(2,1)}, f32[8,128]{1,0:T(8,128)}) custom-call(s32[32]{0:T(128)S(1)} %copy-done.4), custom_call_target="tpu_custom_call" | custom-call | bytes 25165824 | tf_op jit(solution)/shard_map/pallas_call | solution.py:412
  66.6 2.4 %all-to-all-done.1.got_ref = bf16[128,16,128]{2,1,0:T(8,128)(2,1)S(1)} async-done(((bf16[128,16,128]{2,1,0:T(8,128)(2,1)}), bf16[128,16,128]{2,1,0:T(8,128)(2,1)S(1)}, u32[]{:S(2)}, u32[]{:S(2)}) %all-to-all-start.1) | async-done | bytes 524320 | tf_op jit(solution)/shard_map/all_to_all | solution.py:391
  69.0 1.2 copy-done.1
  70.2 0.7 copy-done.5
  70.9 18.4 %shard_map.63 = (f32[32,8,1024]{2,1,0:T(8,128)S(1)}, f32[128,16,128]{2,1,0:T(8,128)S(1)}) custom-call(s32[32]{0:T(128)S(1)} %copy-done.5, bf16[128,16,128]{2,1,0:T(8,128)(2,1)S(1)} %all-to-all-done.1.got_ref, f32[32,8,1024]{2,1,0:T(8,128)S(1)} %copy-done.1, bf16[32,384,1024]{2,1,0:T(8,128)(2,1)} %get-tuple-element.12.fa, ...), custom_call_target="tpu_custom_call" | custom-call | tf_op jit(solution)/shard_map/pallas_call | solution.py:427
  89.3 26.1 %all_to_all.20.got_ref = f32[128,16,128]{2,1,0:T(8,128)S(1)} all-to-all(f32[128,16,128]{2,1,0:T(8,128)S(1)} %get-tuple-element.14), channel_id=1, replica_groups=mesh['group'=8,'patch'=16] {'group','patch'}, dimensions={0} | all-to-all | bytes 2097152 | tf_op jit(solution)/shard_map/all_to_all | solution.py:391
  115.4 1.0 shard_map.64
  116.3 4.7 %all-to-all-start.3 = ((bf16[128,16,128]{2,1,0:T(8,128)(2,1)}), bf16[128,16,128]{2,1,0:T(8,128)(2,1)S(1)}, u32[]{:S(2)}, u32[]{:S(2)}) async-start(bf16[128,16,128]{2,1,0:T(8,128)(2,1)} %get-tuple-element.15), calls=%async_computation.3 | async-start | bytes 1048576 | tf_op jit(solution)/shard_map/all_to_all | solution.py:391
  121.1 0.1 fusion
  121.2 0.1 copy.8
  121.3 0.7 reshape.97
  122.0 13.1 %all-to-all-done.3.got_ref = bf16[128,16,128]{2,1,0:T(8,128)(2,1)S(1)} async-done(((bf16[128,16,128]{2,1,0:T(8,128)(2,1)}), bf16[128,16,128]{2,1,0:T(8,128)(2,1)S(1)}, u32[]{:S(2)}, u32[]{:S(2)}) %all-to-all-start.3) | async-done | bytes 524320 | tf_op jit(solution)/shard_map/all_to_all | solution.py:391
  135.1 10.7 %shard_map.65 = f32[32,8,1024]{2,1,0:T(8,128)} custom-call(s32[32]{0:T(128)S(1)} %copy-done.6, bf16[128,16,128]{2,1,0:T(8,128)(2,1)S(1)} %all-to-all-done.3.got_ref, f32[32,8,1024]{2,1,0:T(8,128)S(1)} %get-tuple-element.16.x_ref, bf16[32,384,1024]{2,1,0:T(8,128)(2,1)} %get-tuple-element.13.fb), custom_call_target="tpu_custom_call" | custom-call | tf_op jit(solution)/shard_map/pallas_call | solution.py:436
  (28 shorter events, 0.6 us)
Async XLA Ops:
  0.6 1.2 copy-start
  1.9 0.7 copy-start.2
  18.9 30.3 %all-to-all-start = ((f32[128,16,128]{2,1,0:T(8,128)}), f32[128,16,128]{2,1,0:T(8,128)S(1)}, u32[]{:S(2)}, u32[]{:S(2)}) async-start(f32[128,16,128]{2,1,0:T(8,128)} %shard_map.59), calls=%async_computation | async-start | bytes 2097152 | tf_op jit(solution)/shard_map/all_to_all | solution.py:391
  30.4 0.7 copy-start.3
  50.2 18.8 %all-to-all-start.1 = ((bf16[128,16,128]{2,1,0:T(8,128)(2,1)}), bf16[128,16,128]{2,1,0:T(8,128)(2,1)S(1)}, u32[]{:S(2)}, u32[]{:S(2)}) async-start(bf16[128,16,128]{2,1,0:T(8,128)(2,1)} %get-tuple-element.11), calls=%async_computation.1 | async-start | bytes 1048576 | tf_op jit(solution)/shard_map/all_to_all | solution.py:391
  55.0 0.7 copy-start.4
  69.0 1.2 copy-start.1
  70.2 0.7 copy-start.5
  70.9 64.2 %copy-start.6 = (s32[32]{0:T(128)S(1)}, s32[32]{0:T(128)}, u32[]{:S(2)}) copy-start(s32[32]{0:T(128)} %place_ref.9) | copy-start | bytes 388
  116.3 18.8 %all-to-all-start.3 = ((bf16[128,16,128]{2,1,0:T(8,128)(2,1)}), bf16[128,16,128]{2,1,0:T(8,128)(2,1)S(1)}, u32[]{:S(2)}, u32[]{:S(2)}) async-start(bf16[128,16,128]{2,1,0:T(8,128)(2,1)} %get-tuple-element.15), calls=%async_computation.3 | async-start | bytes 1048576 | tf_op jit(solution)/shard_map/all_to_all | solution.py:391

commit v2 on v1

--- a/solution.py
+++ b/solution.py
@@ -26,7 +26,9 @@
 CHUNKS = 16
 LOCAL = 32
 DEPTH = 12
+MADE = 8
 TOGETHER = 4
+CODES = 32766.0
 LEAD = 23.75
 
 
@@ -154,8 +156,29 @@
     return (c % 8) * 16 + a * 2 + c // 8
 
 
+def coded(x, unit):
+    root = jnp.sqrt(jnp.sqrt(x))
+    return (root * (CODES / jnp.sqrt(jnp.sqrt(unit))) + 0.5).astype(jnp.int32)
+
+
+def decoded(codes, unit):
+    part = codes * (1.0 / CODES)
+    part = part * part
+    return part * part * unit
+
+
 def write_chunks(out_ref, acc_ref):
     lane4 = lanes(4)
+    largest = jnp.zeros((16, 128), jnp.float32)
+    for a in range(ANG_SUB):
+        for t in range(RAYS // 128):
+            largest = jnp.maximum(largest, acc_ref[a, :, pl.ds(t * 128, 128)])
+    half_unit = jnp.floor(jnp.max(largest[0:8], axis=(0, 1), keepdims=True) * 0.5) + 1.0
+    sum_unit = jnp.floor(jnp.max(largest[8:9], axis=(0, 1), keepdims=True)) + 1.0
+    unit = half_unit * 2.0
+    units = jnp.concatenate(
+        [jnp.broadcast_to(u, (1, 128)).astype(jnp.int32) for u in (half_unit, sum_unit)], axis=0
+    )
     for a in range(ANG_SUB):
         for m in range(CHUNKS // 2):
             for odd in range(2):
@@ -166,12 +189,11 @@
                     half, turned = turned, half
                 packed = jnp.where(lane4 < 64, half[0:4], turned[4:8])
                 sums = jnp.where(lanes(1) < 64, half[8:9], turned[8:9])
-                d = chunk_at(a, 2 * m + odd)
-                out_ref[d, 0:8, :] = whole[0:8]
-                out_ref[d, 8:12, :] = packed
-                out_ref[d, 12:13, :] = whole[8:9]
-                out_ref[d, 13:14, :] = sums
-                out_ref[d, 14:16, :] = jnp.zeros((2, 128), jnp.float32)
+                sums = coded(jnp.concatenate([whole[8:9], sums], axis=0), sum_unit)
+                chunk = jnp.concatenate(
+                    [coded(whole[0:8], unit), coded(packed, unit), sums, units], axis=0
+                )
+                out_ref[chunk_at(a, 2 * m + odd)] = chunk.astype(jnp.int16)
 
 
 def read_chunks(res_ref, got_ref):
@@ -227,29 +249,28 @@
 
 
 def footprint_kernel(subset, place_ref, out_ref, token_ref, slots, l_ref, sems):
-    depth = slots.shape[0]
     token_ref[...] = jnp.zeros_like(token_ref)
     fill_offsets(l_ref, subset)
-    for k in range(depth):
+    for k in range(MADE):
         zero_fill(slots.at[k])
 
-    def step(b, carry):
-        k = lax.rem(b, depth)
-
-        @pl.when(b >= depth)
-        def _():
-            pltpu.make_async_copy(slots.at[k], out_ref.at[b - depth], sems.at[k]).wait()
-
-        at = windows(place_ref, b, subset)
-        for part in range(4):
-            make_footprint(slots.at[k], l_ref, at, subset, part)
-        pltpu.make_async_copy(slots.at[k], out_ref.at[b], sems.at[k]).start()
+    def some(i, carry):
+        for k in range(MADE):
+            b = i * MADE + k
+
+            @pl.when(i > 0)
+            def _():
+                pltpu.make_async_copy(slots.at[k], out_ref.at[b], sems.at[k]).wait()
+
+            at = windows(place_ref, b, subset)
+            for part in range(4):
+                make_footprint(slots.at[k], l_ref, at, subset, part)
+            pltpu.make_async_copy(slots.at[k], out_ref.at[b], sems.at[k]).start()
         return carry
 
-    lax.fori_loop(0, LOCAL, step, 0)
-    for k in range(depth):
-        b = LOCAL - depth + k
-        pltpu.make_async_copy(slots.at[b % depth], out_ref.at[b], sems.at[b % depth]).wait()
+    lax.fori_loop(0, LOCAL // MADE, some, 0)
+    for k in range(MADE):
+        pltpu.make_async_copy(slots.at[k], out_ref.at[LOCAL - MADE + k], sems.at[k]).wait()
 
 
 def streamed(sources, slots, sems, before, step):
@@ -319,13 +340,19 @@
     res_ref, send_ref = refs[-2:]
     count = got_ref.shape[0]
 
+    row = lax.broadcasted_iota(jnp.int32, (16, 128), 0)
+
     def add(i, totals):
-        return tuple(t + got_ref[4 * i + k] for k, t in enumerate(totals))
+        out = []
+        for k, t in enumerate(totals):
+            chunk = got_ref[4 * i + k].astype(jnp.int32).astype(jnp.float32)
+            unit = jnp.where(row < 12, chunk[14:15] * 2.0, chunk[15:16])
+            out.append(t + decoded(chunk, unit))
+        return tuple(out)
 
     zero = jnp.zeros((16, 128), jnp.float32)
     parts = lax.fori_loop(0, count // 4, add, (zero,) * 4, unroll=4)
     total = (parts[0] + parts[1]) + (parts[2] + parts[3])
-    row = lax.broadcasted_iota(jnp.int32, (16, 128), 0)
     sums = jnp.where(row < 8, total[12:13], total[13:14])
     differ = (meas_ref[...] - total / jnp.maximum(sums, 1.0)) * live_ref[...]
     res_ref[...] = differ
@@ -402,7 +429,7 @@
 
     sent = pl.pallas_call(
         first_kernel,
-        out_shape=shape((count, 16, 128)),
+        out_shape=shape((count, 16, 128), jnp.int16),
         in_specs=[SM, VM],
         out_specs=VM,
         scratch_shapes=[F_BUF, F_BUF, L_BUF, ACC_BUF],
@@ -414,7 +441,11 @@
             out_shape=(shape((LOCAL, KALL, VOX), jnp.bfloat16), shape((8, 128))),
             in_specs=[SM],
             out_specs=(ANY, VM),
-            scratch_shapes=[F_RING, L_BUF, pltpu.SemaphoreType.DMA((DEPTH,))],
+            scratch_shapes=[
+                pltpu.VMEM((MADE, KALL, VOX), jnp.bfloat16),
+                L_BUF,
+                pltpu.SemaphoreType.DMA((MADE,)),
+            ],
             compiler_params=PARAMS,
             cost_estimate=pl.CostEstimate(
                 flops=0, bytes_accessed=LOCAL * KALL * VOX * 2, transcendentals=0
@@ -426,7 +457,7 @@
     fb, _ = footprints(1)
     estimate, sent = pl.pallas_call(
         middle_kernel,
-        out_shape=(shape(volume.shape), shape((count, 16, 128))),
+        out_shape=(shape(volume.shape), shape((count, 16, 128), jnp.int16)),
         in_specs=[SM, VM, VM, ANY, ANY],
         out_specs=(VM, VM),
         scratch_shapes=[F_RING, F_RING, ACC_BUF, RES_BUF, pltpu.SemaphoreType.DMA((2, DEPTH))],

time: 146 us -> 142 us (0.973)
  blocking collectives: 26.1 us -> 20.7 us
  waiting for transfers between devices: 20.4 us -> 16.5 us
  starting transfers between devices: 21 us -> 24.8 us
    all_to_all x1, blocking collectives: 26.1 us -> 20.7 us  [exchanged(): return lax.all_to_all(sent, axes, 0, 0, tiled=True)]
    all_to_all x3, waiting for transfers between devices: 20.4 us -> 16.5 us  [exchanged(): return lax.all_to_all(sent, axes, 0, 0, tiled=True)]
    all_to_all x3, starting transfers between devices: 21 us -> 24.8 us  [exchanged(): return lax.all_to_all(sent, axes, 0, 0, tiled=True)]
  transfers between devices with their start and end apart: 3 -> 3, of which waited for: 3 -> 3; matrix products, arithmetic and copies ran while one was open for 3% -> 3% of each run, Pallas kernels for 15% -> 14%
where the time goes in v2:
time: 142 us
  Pallas kernels  69.8 us (49%)
  starting transfers between devices  24.8 us (17%)
  blocking collectives  20.7 us (15%)
  waiting for transfers between devices  16.5 us (12%)
  local copies, waits for them, and re-layouts  8.32 us (6%)
    all_to_all x3, starting transfers between devices, exchanged(): return lax.all_to_all(sent, axes, 0, 0, tiled=True)  24.8 us
    all_to_all x1, blocking collectives, exchanged(): return lax.all_to_all(sent, axes, 0, 0, tiled=True)  20.7 us
    pallas_call x2, Pallas kernels, footprints(): pl.pallas_call(functools.partial(footprint_kernel, subset), out_shape=(sh...  20.3 us
    pallas_call x1, Pallas kernels, shards(): pl.pallas_call(middle_kernel, out_shape=(shape(volume.shape), shape((coun...  19.3 us
    pallas_call x1, Pallas kernels, shards(): pl.pallas_call(first_kernel, out_shape=shape((count, 16, 128), jnp.int16)...  17 us
    all_to_all x3, waiting for transfers between devices, exchanged(): return lax.all_to_all(sent, axes, 0, 0, tiled=True)  16.5 us
    pallas_call x1, Pallas kernels, shards(): pl.pallas_call(last_kernel, out_shape=shape(volume.shape), in_specs=[SM,...  10.7 us
    unnamed x14, local copies, waits for them, and re-layouts  5.07 us
  transfers between devices with their start and end apart: 3, of which 3 were waited for; matrix products, arithmetic and copies ran while one was open for 3% of the time, Pallas kernels for 14%

profile of v2, /device:TPU:1, one launch (start us, length us, event | category | flops | bytes accessed | tf_op | source)
XLA Modules:
  0.0 141.5 jit_solution(7908481166634663334)
XLA Ops:
  0.6 1.2 copy-done
  1.9 0.7 copy-done.2
  2.5 17.0 %shard_map.59 = s16[128,16,128]{2,1,0:T(8,128)(2,1)} custom-call(s32[32]{0:T(128)S(1)} %copy-done.2, f32[32,8,1024]{2,1,0:T(8,128)S(1)} %copy-done), custom_call_target="tpu_custom_call" | custom-call | tf_op jit(solution)/shard_map/pallas_call | solution.py:430
  19.5 11.5 %all-to-all-start = ((s16[128,16,128]{2,1,0:T(8,128)(2,1)}), s16[128,16,128]{2,1,0:T(8,128)(2,1)S(1)}, u32[]{:S(2)}, u32[]{:S(2)}) async-start(s16[128,16,128]{2,1,0:T(8,128)(2,1)} %shard_map.59), calls=%async_computation | async-start | bytes 1048576 | tf_op jit(solution)/shard_map/all_to_all | solution.py:418
  31.0 0.8 fusion.11
  32.0 0.1 reshape.98
  32.2 0.1 reshape.99
  32.3 0.8 fusion.9
  33.1 0.1 reshape.95
  33.3 0.1 reshape.96
  33.5 0.1 fusion.3
  33.6 0.7 copy-done.3
  34.2 9.8 %shard_map.60 = (bf16[32,384,1024]{2,1,0:T(8,128)(2,1)}, f32[8,128]{1,0:T(8,128)S(1)}) custom-call(s32[32]{0:T(128)S(1)} %copy-done.3), custom_call_target="tpu_custom_call" | custom-call | bytes 25165824 | tf_op jit(solution)/shard_map/pallas_call | solution.py:439
  44.1 0.1 pad.21.clone
  44.2 0.1 maximum_maximum_fusion.3
  44.3 0.6 all-to-all-done.got_ref
  44.9 1.2 shard_map.61
  46.2 9.1 %all-to-all-start.1 = ((bf16[128,16,128]{2,1,0:T(8,128)(2,1)}), bf16[128,16,128]{2,1,0:T(8,128)(2,1)S(1)}, u32[]{:S(2)}, u32[]{:S(2)}) async-start(bf16[128,16,128]{2,1,0:T(8,128)(2,1)} %get-tuple-element.11), calls=%async_computation.1 | async-start | bytes 1048576 | tf_op jit(solution)/shard_map/all_to_all | solution.py:418
  55.3 0.6 copy-done.4
  56.0 10.5 %shard_map.62 = (bf16[32,384,1024]{2,1,0:T(8,128)(2,1)}, f32[8,128]{1,0:T(8,128)}) custom-call(s32[32]{0:T(128)S(1)} %copy-done.4), custom_call_target="tpu_custom_call" | custom-call | bytes 25165824 | tf_op jit(solution)/shard_map/pallas_call | solution.py:439
  66.5 2.8 %all-to-all-done.1.got_ref = bf16[128,16,128]{2,1,0:T(8,128)(2,1)S(1)} async-done(((bf16[128,16,128]{2,1,0:T(8,128)(2,1)}), bf16[128,16,128]{2,1,0:T(8,128)(2,1)S(1)}, u32[]{:S(2)}, u32[]{:S(2)}) %all-to-all-start.1) | async-done | bytes 524320 | tf_op jit(solution)/shard_map/all_to_all | solution.py:418
  69.2 1.2 copy-done.1
  70.5 0.7 copy-done.5
  71.1 19.3 %shard_map.63 = (f32[32,8,1024]{2,1,0:T(8,128)S(1)}, s16[128,16,128]{2,1,0:T(8,128)(2,1)S(1)}) custom-call(s32[32]{0:T(128)S(1)} %copy-done.5, bf16[128,16,128]{2,1,0:T(8,128)(2,1)S(1)} %all-to-all-done.1.got_ref, f32[32,8,1024]{2,1,0:T(8,128)S(1)} %copy-done.1, bf16[32,384,1024]{2,1,0:T(8,128)(2,1)} %get-tuple-element.12.fa, ...), custom_call_target="tpu_custom_call" | custom-call | tf_op jit(solution)/shard_map/pallas_call | solution.py:458
  90.4 20.7 %all_to_all.20.got_ref = s16[128,16,128]{2,1,0:T(8,128)(2,1)S(1)} all-to-all(s16[128,16,128]{2,1,0:T(8,128)(2,1)S(1)} %get-tuple-element.14), channel_id=1, replica_groups=mesh['group'=8,'patch'=16] {'group','patch'}, dimensions={0} | all-to-all | bytes 1048576 | tf_op jit(solution)/shard_map/all_to_all | solution.py:418
  111.2 1.2 shard_map.64
  112.4 4.2 %all-to-all-start.3 = ((bf16[128,16,128]{2,1,0:T(8,128)(2,1)}), bf16[128,16,128]{2,1,0:T(8,128)(2,1)S(1)}, u32[]{:S(2)}, u32[]{:S(2)}) async-start(bf16[128,16,128]{2,1,0:T(8,128)(2,1)} %get-tuple-element.15), calls=%async_computation.3 | async-start | bytes 1048576 | tf_op jit(solution)/shard_map/all_to_all | solution.py:418
  116.7 0.1 fusion
  116.8 0.1 copy.8
  116.9 0.7 reshape.97
  117.6 13.1 %all-to-all-done.3.got_ref = bf16[128,16,128]{2,1,0:T(8,128)(2,1)S(1)} async-done(((bf16[128,16,128]{2,1,0:T(8,128)(2,1)}), bf16[128,16,128]{2,1,0:T(8,128)(2,1)S(1)}, u32[]{:S(2)}, u32[]{:S(2)}) %all-to-all-start.3) | async-done | bytes 524320 | tf_op jit(solution)/shard_map/all_to_all | solution.py:418
  130.6 10.7 %shard_map.65 = f32[32,8,1024]{2,1,0:T(8,128)} custom-call(s32[32]{0:T(128)S(1)} %copy-done.6, bf16[128,16,128]{2,1,0:T(8,128)(2,1)S(1)} %all-to-all-done.3.got_ref, f32[32,8,1024]{2,1,0:T(8,128)S(1)} %get-tuple-element.16.x_ref, bf16[32,384,1024]{2,1,0:T(8,128)(2,1)} %get-tuple-element.13.fb), custom_call_target="tpu_custom_call" | custom-call | tf_op jit(solution)/shard_map/pallas_call | solution.py:467
  (28 shorter events, 0.6 us)
Async XLA Ops:
  0.6 1.2 copy-start
  1.9 0.7 copy-start.2
  19.5 25.4 %all-to-all-start = ((s16[128,16,128]{2,1,0:T(8,128)(2,1)}), s16[128,16,128]{2,1,0:T(8,128)(2,1)S(1)}, u32[]{:S(2)}, u32[]{:S(2)}) async-start(s16[128,16,128]{2,1,0:T(8,128)(2,1)} %shard_map.59), calls=%async_computation | async-start | bytes 1048576 | tf_op jit(solution)/shard_map/all_to_all | solution.py:418
  33.6 0.7 copy-start.3
  46.2 23.1 %all-to-all-start.1 = ((bf16[128,16,128]{2,1,0:T(8,128)(2,1)}), bf16[128,16,128]{2,1,0:T(8,128)(2,1)S(1)}, u32[]{:S(2)}, u32[]{:S(2)}) async-start(bf16[128,16,128]{2,1,0:T(8,128)(2,1)} %get-tuple-element.11), calls=%async_computation.1 | async-start | bytes 1048576 | tf_op jit(solution)/shard_map/all_to_all | solution.py:418
  55.3 0.7 copy-start.4
  69.2 1.2 copy-start.1
  70.5 0.7 copy-start.5
  71.1 59.5 %copy-start.6 = (s32[32]{0:T(128)S(1)}, s32[32]{0:T(128)}, u32[]{:S(2)}) copy-start(s32[32]{0:T(128)} %place_ref.9) | copy-start | bytes 388
  112.4 18.2 %all-to-all-start.3 = ((bf16[128,16,128]{2,1,0:T(8,128)(2,1)}), bf16[128,16,128]{2,1,0:T(8,128)(2,1)S(1)}, u32[]{:S(2)}, u32[]{:S(2)}) async-start(bf16[128,16,128]{2,1,0:T(8,128)(2,1)} %get-tuple-element.15), calls=%async_computation.3 | async-start | bytes 1048576 | tf_op jit(solution)/shard_map/all_to_all | solution.py:418

commit v3 on v2

--- a/solution.py
+++ b/solution.py
@@ -248,7 +248,8 @@
     return jnp.maximum(x + total[0:8] * (RELAX / total[8:9]), 0.0)
 
 
-def footprint_kernel(subset, place_ref, out_ref, token_ref, slots, l_ref, sems):
+def footprint_kernel(subset, start, place_ref, *refs):
+    out_ref, token_ref, slots, l_ref, sems = refs[-5:]
     token_ref[...] = jnp.zeros_like(token_ref)
     fill_offsets(l_ref, subset)
     for k in range(MADE):
@@ -256,7 +257,7 @@
 
     def some(i, carry):
         for k in range(MADE):
-            b = i * MADE + k
+            b = start + i * MADE + k
 
             @pl.when(i > 0)
             def _():
@@ -268,9 +269,10 @@
             pltpu.make_async_copy(slots.at[k], out_ref.at[b], sems.at[k]).start()
         return carry
 
-    lax.fori_loop(0, LOCAL // MADE, some, 0)
+    lax.fori_loop(0, LOCAL // 2 // MADE, some, 0)
     for k in range(MADE):
-        pltpu.make_async_copy(slots.at[k], out_ref.at[LOCAL - MADE + k], sems.at[k]).wait()
+        b = start + LOCAL // 2 - MADE + k
+        pltpu.make_async_copy(slots.at[k], out_ref.at[b], sems.at[k]).wait()
 
 
 def streamed(sources, slots, sems, before, step):
@@ -299,28 +301,45 @@
                 copy(n, first + k).wait()
         for k in range(TOGETHER):
             b = first + k
-            step(b, [slots[n].at[lax.rem(b, DEPTH)] for n in many])
+            step(b, k, [slots[n].at[lax.rem(b, DEPTH)] for n in many])
         return carry
 
     lax.fori_loop(0, LOCAL // TOGETHER, some, 0)
 
 
 def middle_kernel(
-    place_ref, got_ref, x_ref, fa, fb, new_ref, out_ref, a_slots, b_slots, acc_ref, res_ref, sems
+    place_ref, got_ref, x_ref, fa, new_ref, out_ref, ring, g0, g1, l_ref, acc_ref, res_ref, sems
 ):
+    made = (g0, g1)
+
+    def make(f, b):
+        at = windows(place_ref, b, 1)
+        return lambda part: make_footprint(f, l_ref, at, 1, part)
+
     def before():
+        fill_offsets(l_ref, 1)
+        zero_fill(g0)
+        zero_fill(g1)
+        for part in range(4):
+            make(g0, 0)(part)
         read_chunks(res_ref, got_ref)
         acc_ref[...] = jnp.zeros_like(acc_ref)
 
-    def step(b, refs):
+    def step(b, k, refs):
+        f = made[k % 2]
+        fill = make(made[(k + 1) % 2], jnp.minimum(b + 1, LOCAL - 1))
         res = gather_windows(res_ref, windows(place_ref, b, 0))
         total = jnp.dot(res, refs[0][...], preferred_element_type=jnp.float32)
         x = updated(x_ref[b], total)
         new_ref[b] = x
         x = with_ones(x)
-        scatter_windows(acc_ref, project(x, refs[1]), windows(place_ref, b, 1))
-
-    streamed((fa, fb), (a_slots, b_slots), sems, before, step)
+        contrib = 0.0
+        for part in range(4):
+            contrib = contrib + project(x, f, slice(part * 256, part * 256 + 256))
+            fill(part)
+        scatter_windows(acc_ref, contrib, windows(place_ref, b, 1))
+
+    streamed((fa,), (ring,), sems, before, step)
     write_chunks(out_ref, acc_ref)
 
 
@@ -328,7 +347,7 @@
     def before():
         read_chunks(res_ref, got_ref)
 
-    def step(b, refs):
+    def step(b, k, refs):
         res = gather_windows(res_ref, windows(place_ref, b, 1))
         total = jnp.dot(res, refs[0][...], preferred_element_type=jnp.float32)
         new_ref[b] = updated(x_ref[b], total)
@@ -435,35 +454,46 @@
         scratch_shapes=[F_BUF, F_BUF, L_BUF, ACC_BUF],
         compiler_params=PARAMS,
     )(block_place, volume)
-    def footprints(subset):
+    def footprints(subset, start, *held):
         return pl.pallas_call(
-            functools.partial(footprint_kernel, subset),
+            functools.partial(footprint_kernel, subset, start),
             out_shape=(shape((LOCAL, KALL, VOX), jnp.bfloat16), shape((8, 128))),
-            in_specs=[SM],
+            in_specs=[SM] + [ANY] * len(held),
             out_specs=(ANY, VM),
             scratch_shapes=[
                 pltpu.VMEM((MADE, KALL, VOX), jnp.bfloat16),
                 L_BUF,
                 pltpu.SemaphoreType.DMA((MADE,)),
             ],
+            input_output_aliases={1: 0} if held else {},
             compiler_params=PARAMS,
             cost_estimate=pl.CostEstimate(
-                flops=0, bytes_accessed=LOCAL * KALL * VOX * 2, transcendentals=0
+                flops=0, bytes_accessed=LOCAL * KALL * VOX, transcendentals=0
             ),
-        )(block_place)
-
-    fa, token = footprints(0)
+        )(block_place, *held)
+
+    fa, token = footprints(0, 0)
     _, rounded = residual(sent, 0, token)
-    fb, _ = footprints(1)
+    fa, _ = footprints(0, LOCAL // 2, fa)
     estimate, sent = pl.pallas_call(
         middle_kernel,
         out_shape=(shape(volume.shape), shape((count, 16, 128), jnp.int16)),
-        in_specs=[SM, VM, VM, ANY, ANY],
+        in_specs=[SM, VM, VM, ANY],
         out_specs=(VM, VM),
-        scratch_shapes=[F_RING, F_RING, ACC_BUF, RES_BUF, pltpu.SemaphoreType.DMA((2, DEPTH))],
+        scratch_shapes=[
+            F_RING,
+            F_BUF,
+            F_BUF,
+            L_BUF,
+            ACC_BUF,
+            RES_BUF,
+            pltpu.SemaphoreType.DMA((1, DEPTH)),
+        ],
         compiler_params=PARAMS,
-    )(block_place, exchanged(rounded), volume, fa, fb)
-    last, rounded = residual(sent, 1)
+    )(block_place, exchanged(rounded), volume, fa)
+    fb, token = footprints(1, 0)
+    last, rounded = residual(sent, 1, token)
+    fb, _ = footprints(1, LOCAL // 2, fb)
     final = pl.pallas_call(
         last_kernel,
         out_shape=shape(volume.shape),

time: 142 us -> 139 us (0.979)
  blocking collectives: 20.7 us -> 0 us
  Pallas kernels: 69.8 us -> 79.8 us
  waiting for transfers between devices: 16.5 us -> 25.9 us
  local copies, waits for them, and re-layouts: 8.32 us -> 6.45 us
    all_to_all x1 -> x0, blocking collectives: 20.7 us -> none  [exchanged(): return lax.all_to_all(sent, axes, 0, 0, tiled=True)]
    all_to_all x3 -> x4, waiting for transfers between devices: 16.5 us -> 25.9 us  [exchanged(): return lax.all_to_all(sent, axes, 0, 0, tiled=True)]
    pallas_call x1, Pallas kernels: 19.3 us -> 24.7 us  [shards(): pl.pallas_call(middle_kernel, out_shape=(shape(volume.shape), shape((coun...]
    pallas_call x2 -> x4, Pallas kernels: 20.3 us -> 24.9 us  [footprints(): pl.pallas_call(functools.partial(footprint_kernel, subset, start), out_sh...]
    unnamed x14 -> x12, local copies, waits for them, and re-layouts: 5.07 us -> 3.19 us
    all_to_all x3 -> x4, starting transfers between devices: 24.8 us -> 25.1 us  [exchanged(): return lax.all_to_all(sent, axes, 0, 0, tiled=True)]
  transfers between devices with their start and end apart: 3 -> 4, of which waited for: 3 -> 4; matrix products, arithmetic and copies ran while one was open for 3% -> 3% of each run, Pallas kernels for 14% -> 18%
where the time goes in v3:
time: 139 us
  Pallas kernels  79.8 us (57%)
  waiting for transfers between devices  25.9 us (19%)
  starting transfers between devices  25.1 us (18%)
  local copies, waits for them, and re-layouts  6.45 us (5%)
    all_to_all x4, waiting for transfers between devices, exchanged(): return lax.all_to_all(sent, axes, 0, 0, tiled=True)  25.9 us
    all_to_all x4, starting transfers between devices, exchanged(): return lax.all_to_all(sent, axes, 0, 0, tiled=True)  25.1 us
    pallas_call x4, Pallas kernels, footprints(): pl.pallas_call(functools.partial(footprint_kernel, subset, start), out_sh...  24.9 us
    pallas_call x1, Pallas kernels, shards(): pl.pallas_call(middle_kernel, out_shape=(shape(volume.shape), shape((coun...  24.7 us
    pallas_call x1, Pallas kernels, shards(): pl.pallas_call(first_kernel, out_shape=shape((count, 16, 128), jnp.int16)...  17 us
    pallas_call x1, Pallas kernels, shards(): pl.pallas_call(last_kernel, out_shape=shape(volume.shape), in_specs=[SM,...  10.7 us
    unnamed x12, local copies, waits for them, and re-layouts  3.19 us
  transfers between devices with their start and end apart: 4, of which 4 were waited for; matrix products, arithmetic and copies ran while one was open for 3% of the time, Pallas kernels for 18%

profile of v3, /device:TPU:1, one launch (start us, length us, event | category | flops | bytes accessed | tf_op | source)
XLA Modules:
  0.0 138.7 jit_solution(18210656843795172649)
XLA Ops:
  0.6 1.2 copy-done
  1.9 0.7 copy-done.2
  2.5 17.0 %shard_map.59 = s16[128,16,128]{2,1,0:T(8,128)(2,1)} custom-call(s32[32]{0:T(128)S(1)} %copy-done.2, f32[32,8,1024]{2,1,0:T(8,128)S(1)} %copy-done), custom_call_target="tpu_custom_call" | custom-call | tf_op jit(solution)/shard_map/pallas_call | solution.py:449
  19.5 11.5 %all-to-all-start = ((s16[128,16,128]{2,1,0:T(8,128)(2,1)}), s16[128,16,128]{2,1,0:T(8,128)(2,1)S(1)}, u32[]{:S(2)}, u32[]{:S(2)}) async-start(s16[128,16,128]{2,1,0:T(8,128)(2,1)} %shard_map.59), calls=%async_computation | async-start | bytes 1048576 | tf_op jit(solution)/shard_map/all_to_all | solution.py:437
  31.0 0.8 fusion.9
  31.9 0.1 reshape.95
  32.1 0.1 reshape.96
  32.3 0.8 fusion.11
  33.2 0.1 reshape.98
  33.4 0.1 reshape.99
  33.5 0.1 fusion.3
  33.6 0.7 copy-done.3
  34.3 5.9 %shard_map.60 = (bf16[32,384,1024]{2,1,0:T(8,128)(2,1)}, f32[8,128]{1,0:T(8,128)S(1)}) custom-call(s32[32]{0:T(128)S(1)} %copy-done.3), custom_call_target="tpu_custom_call" | custom-call | bytes 12582912 | tf_op jit(solution)/shard_map/pallas_call | solution.py:458
  40.3 0.1 maximum_maximum_fusion.3
  40.4 4.5 %all-to-all-done.got_ref = s16[128,16,128]{2,1,0:T(8,128)(2,1)S(1)} async-done(((s16[128,16,128]{2,1,0:T(8,128)(2,1)}), s16[128,16,128]{2,1,0:T(8,128)(2,1)S(1)}, u32[]{:S(2)}, u32[]{:S(2)}) %all-to-all-start) | async-done | bytes 524320 | tf_op jit(solution)/shard_map/all_to_all | solution.py:437
  44.9 1.2 shard_map.61
  46.2 5.2 %all-to-all-start.1 = ((bf16[128,16,128]{2,1,0:T(8,128)(2,1)}), bf16[128,16,128]{2,1,0:T(8,128)(2,1)S(1)}, u32[]{:S(2)}, u32[]{:S(2)}) async-start(bf16[128,16,128]{2,1,0:T(8,128)(2,1)} %get-tuple-element.14), calls=%async_computation.1 | async-start | bytes 1048576 | tf_op jit(solution)/shard_map/all_to_all | solution.py:437
  51.4 0.6 copy-done.4
  52.1 6.5 %shard_map.62 = (bf16[32,384,1024]{2,1,0:T(8,128)(2,1)}, f32[8,128]{1,0:T(8,128)}) custom-call(s32[32]{0:T(128)S(1)} %copy-done.4, bf16[32,384,1024]{2,1,0:T(8,128)(2,1)} %get-tuple-element.15.refs_0_), custom_call_target="tpu_custom_call", output_to_operand_aliasing={{0}: (1, {})} | custom-call | bytes 12582912 | tf_op jit(solution)/shard_map/pallas_call | solution.py:458
  58.6 6.7 %all-to-all-done.1.got_ref = bf16[128,16,128]{2,1,0:T(8,128)(2,1)S(1)} async-done(((bf16[128,16,128]{2,1,0:T(8,128)(2,1)}), bf16[128,16,128]{2,1,0:T(8,128)(2,1)S(1)}, u32[]{:S(2)}, u32[]{:S(2)}) %all-to-all-start.1) | async-done | bytes 524320 | tf_op jit(solution)/shard_map/all_to_all | solution.py:437
  65.3 24.7 %shard_map.63 = (f32[32,8,1024]{2,1,0:T(8,128)S(1)}, s16[128,16,128]{2,1,0:T(8,128)(2,1)}) custom-call(s32[32]{0:T(128)S(1)} %copy-done.5, bf16[128,16,128]{2,1,0:T(8,128)(2,1)S(1)} %all-to-all-done.1.got_ref, f32[32,8,1024]{2,1,0:T(8,128)S(1)} %copy-done.1, bf16[32,384,1024]{2,1,0:T(8,128)(2,1)} %get-tuple-element.16.fa), custom_call_target="tpu_custom_call" | custom-call | tf_op jit(solution)/shard_map/pallas_call | solution.py:478
  90.0 4.2 %all-to-all-start.2 = ((s16[128,16,128]{2,1,0:T(8,128)(2,1)}), s16[128,16,128]{2,1,0:T(8,128)(2,1)S(1)}, u32[]{:S(2)}, u32[]{:S(2)}) async-start(s16[128,16,128]{2,1,0:T(8,128)(2,1)} %get-tuple-element.17), calls=%async_computation.2 | async-start | bytes 1048576 | tf_op jit(solution)/shard_map/all_to_all | solution.py:437
  94.2 5.9 %shard_map.64 = (bf16[32,384,1024]{2,1,0:T(8,128)(2,1)}, f32[8,128]{1,0:T(8,128)S(1)}) custom-call(s32[32]{0:T(128)S(1)} %copy-done.5), custom_call_target="tpu_custom_call" | custom-call | bytes 12582912 | tf_op jit(solution)/shard_map/pallas_call | solution.py:458
  100.2 8.1 %all-to-all-done.2.got_ref = s16[128,16,128]{2,1,0:T(8,128)(2,1)S(1)} async-done(((s16[128,16,128]{2,1,0:T(8,128)(2,1)}), s16[128,16,128]{2,1,0:T(8,128)(2,1)S(1)}, u32[]{:S(2)}, u32[]{:S(2)}) %all-to-all-start.2) | async-done | bytes 524320 | tf_op jit(solution)/shard_map/all_to_all | solution.py:437
  108.3 1.2 shard_map.65
  109.5 4.2 %all-to-all-start.3 = ((bf16[128,16,128]{2,1,0:T(8,128)(2,1)}), bf16[128,16,128]{2,1,0:T(8,128)(2,1)S(1)}, u32[]{:S(2)}, u32[]{:S(2)}) async-start(bf16[128,16,128]{2,1,0:T(8,128)(2,1)} %get-tuple-element.19), calls=%async_computation.3 | async-start | bytes 1048576 | tf_op jit(solution)/shard_map/all_to_all | solution.py:437
  113.7 6.6 %shard_map.66 = (bf16[32,384,1024]{2,1,0:T(8,128)(2,1)}, f32[8,128]{1,0:T(8,128)}) custom-call(s32[32]{0:T(128)S(1)} %copy-done.5, bf16[32,384,1024]{2,1,0:T(8,128)(2,1)} %get-tuple-element.21.refs_0_), custom_call_target="tpu_custom_call", output_to_operand_aliasing={{0}: (1, {})} | custom-call | bytes 12582912 | tf_op jit(solution)/shard_map/pallas_call | solution.py:458
  120.4 0.1 fusion
  120.5 0.1 copy.10
  120.6 0.7 reshape.97
  121.3 6.5 %all-to-all-done.3.got_ref = bf16[128,16,128]{2,1,0:T(8,128)(2,1)S(1)} async-done(((bf16[128,16,128]{2,1,0:T(8,128)(2,1)}), bf16[128,16,128]{2,1,0:T(8,128)(2,1)S(1)}, u32[]{:S(2)}, u32[]{:S(2)}) %all-to-all-start.3) | async-done | bytes 524320 | tf_op jit(solution)/shard_map/all_to_all | solution.py:437
  127.8 10.7 %shard_map.67 = f32[32,8,1024]{2,1,0:T(8,128)} custom-call(s32[32]{0:T(128)S(1)} %copy-done.5, bf16[128,16,128]{2,1,0:T(8,128)(2,1)S(1)} %all-to-all-done.3.got_ref, f32[32,8,1024]{2,1,0:T(8,128)S(1)} %get-tuple-element.20.x_ref, bf16[32,384,1024]{2,1,0:T(8,128)(2,1)} %get-tuple-element.22.fb), custom_call_target="tpu_custom_call" | custom-call | tf_op jit(solution)/shard_map/pallas_call | solution.py:497
  (29 shorter events, 0.7 us)
Async XLA Ops:
  0.6 1.2 copy-start
  1.9 0.7 copy-start.2
  2.5 62.8 %copy-start.1 = (f32[32,8,1024]{2,1,0:T(8,128)S(1)}, f32[32,8,1024]{2,1,0:T(8,128)}, u32[]{:S(2)}) copy-start(f32[32,8,1024]{2,1,0:T(8,128)} %x_ref.3) | copy-start | bytes 3145732
  2.5 62.8 %copy-start.5 = (s32[32]{0:T(128)S(1)}, s32[32]{0:T(128)}, u32[]{:S(2)}) copy-start(s32[32]{0:T(128)} %place_ref.13) | copy-start | bytes 388
  19.5 25.4 %all-to-all-start = ((s16[128,16,128]{2,1,0:T(8,128)(2,1)}), s16[128,16,128]{2,1,0:T(8,128)(2,1)S(1)}, u32[]{:S(2)}, u32[]{:S(2)}) async-start(s16[128,16,128]{2,1,0:T(8,128)(2,1)} %shard_map.59), calls=%async_computation | async-start | bytes 1048576 | tf_op jit(solution)/shard_map/all_to_all | solution.py:437
  33.6 0.7 copy-start.3
  46.2 19.1 %all-to-all-start.1 = ((bf16[128,16,128]{2,1,0:T(8,128)(2,1)}), bf16[128,16,128]{2,1,0:T(8,128)(2,1)S(1)}, u32[]{:S(2)}, u32[]{:S(2)}) async-start(bf16[128,16,128]{2,1,0:T(8,128)(2,1)} %get-tuple-element.14), calls=%async_computation.1 | async-start | bytes 1048576 | tf_op jit(solution)/shard_map/all_to_all | solution.py:437
  51.4 0.7 copy-start.4
  90.0 18.3 %all-to-all-start.2 = ((s16[128,16,128]{2,1,0:T(8,128)(2,1)}), s16[128,16,128]{2,1,0:T(8,128)(2,1)S(1)}, u32[]{:S(2)}, u32[]{:S(2)}) async-start(s16[128,16,128]{2,1,0:T(8,128)(2,1)} %get-tuple-element.17), calls=%async_computation.2 | async-start | bytes 1048576 | tf_op jit(solution)/shard_map/all_to_all | solution.py:437
  109.5 18.2 %all-to-all-start.3 = ((bf16[128,16,128]{2,1,0:T(8,128)(2,1)}), bf16[128,16,128]{2,1,0:T(8,128)(2,1)S(1)}, u32[]{:S(2)}, u32[]{:S(2)}) async-start(bf16[128,16,128]{2,1,0:T(8,128)(2,1)} %get-tuple-element.19), calls=%async_computation.3 | async-start | bytes 1048576 | tf_op jit(solution)/shard_map/all_to_all | solution.py:437

commit v4 on v3

--- a/solution.py
+++ b/solution.py
@@ -26,7 +26,7 @@
 CHUNKS = 16
 LOCAL = 32
 DEPTH = 12
-MADE = 8
+MADE = 4
 TOGETHER = 4
 CODES = 32766.0
 LEAD = 23.75
@@ -156,9 +156,9 @@
     return (c % 8) * 16 + a * 2 + c // 8
 
 
-def coded(x, unit):
-    root = jnp.sqrt(jnp.sqrt(x))
-    return (root * (CODES / jnp.sqrt(jnp.sqrt(unit))) + 0.5).astype(jnp.int32)
+def coded(x, scale):
+    root = lax.rsqrt(lax.rsqrt(jnp.maximum(x, 1e-30)))
+    return (root * scale + 0.5).astype(jnp.int32)
 
 
 def decoded(codes, unit):
@@ -175,10 +175,10 @@
             largest = jnp.maximum(largest, acc_ref[a, :, pl.ds(t * 128, 128)])
     half_unit = jnp.floor(jnp.max(largest[0:8], axis=(0, 1), keepdims=True) * 0.5) + 1.0
     sum_unit = jnp.floor(jnp.max(largest[8:9], axis=(0, 1), keepdims=True)) + 1.0
-    unit = half_unit * 2.0
-    units = jnp.concatenate(
-        [jnp.broadcast_to(u, (1, 128)).astype(jnp.int32) for u in (half_unit, sum_unit)], axis=0
-    )
+    scale, sum_scale = (CODES * lax.rsqrt(jnp.sqrt(u)) for u in (half_unit * 2.0, sum_unit))
+    row = lax.broadcasted_iota(jnp.int32, (8, 128), 0)
+    mixed = jnp.where(row < 4, scale, sum_scale)
+    units = jnp.where(row == 6, half_unit, sum_unit).astype(jnp.int32)
     for a in range(ANG_SUB):
         for m in range(CHUNKS // 2):
             for odd in range(2):
@@ -189,10 +189,9 @@
                     half, turned = turned, half
                 packed = jnp.where(lane4 < 64, half[0:4], turned[4:8])
                 sums = jnp.where(lanes(1) < 64, half[8:9], turned[8:9])
-                sums = coded(jnp.concatenate([whole[8:9], sums], axis=0), sum_unit)
-                chunk = jnp.concatenate(
-                    [coded(whole[0:8], unit), coded(packed, unit), sums, units], axis=0
-                )
+                rest = jnp.concatenate([packed, whole[8:9], sums, sums, sums], axis=0)
+                rest = jnp.where(row < 6, coded(rest, mixed), units)
+                chunk = jnp.concatenate([coded(whole[0:8], scale), rest], axis=0)
                 out_ref[chunk_at(a, 2 * m + odd)] = chunk.astype(jnp.int16)
 
 
@@ -210,22 +209,12 @@
         res_ref[a, :, pl.ds(RAYS, 128)] = jnp.zeros((8, 128), jnp.float32)
 
 
-def two_slots(step, f0, f1, make):
-    for part in range(4):
-        make(f0, 0)(part)
-
-    def both(i, carry):
-        step(2 * i, f0, make(f1, 2 * i + 1))
-        step(2 * i + 1, f1, make(f0, jnp.minimum(2 * i + 2, LOCAL - 1)))
-        return carry
-
-    lax.fori_loop(0, LOCAL // 2, both, 0)
-
-
-def first_kernel(place_ref, x_ref, out_ref, f0, f1, l_ref, acc_ref):
+def first_kernel(place_ref, x_ref, out_ref, *refs):
+    slots, (l_ref, acc_ref) = refs[:-2], refs[-2:]
+    count = len(slots)
     fill_offsets(l_ref, 0)
-    zero_fill(f0)
-    zero_fill(f1)
+    for f in slots:
+        zero_fill(f)
     acc_ref[...] = jnp.zeros_like(acc_ref)
 
     def make(f, b):
@@ -240,7 +229,16 @@
             fill(part)
         scatter_windows(acc_ref, contrib, windows(place_ref, b, 0))
 
-    two_slots(step, f0, f1, make)
+    for part in range(4):
+        make(slots[0], 0)(part)
+
+    def some(i, carry):
+        for k in range(count):
+            b = i * count + k
+            step(b, slots[k], make(slots[(k + 1) % count], jnp.minimum(b + 1, LOCAL - 1)))
+        return carry
+
+    lax.fori_loop(0, LOCAL // count, some, 0)
     write_chunks(out_ref, acc_ref)
 
 
@@ -308,9 +306,9 @@
 
 
 def middle_kernel(
-    place_ref, got_ref, x_ref, fa, new_ref, out_ref, ring, g0, g1, l_ref, acc_ref, res_ref, sems
+    place_ref, got_ref, x_ref, fa, new_ref, out_ref, ring, l_ref, acc_ref, res_ref, sems, *made
 ):
-    made = (g0, g1)
+    count = len(made)
 
     def make(f, b):
         at = windows(place_ref, b, 1)
@@ -318,16 +316,16 @@
 
     def before():
         fill_offsets(l_ref, 1)
-        zero_fill(g0)
-        zero_fill(g1)
+        for f in made:
+            zero_fill(f)
         for part in range(4):
-            make(g0, 0)(part)
+            make(made[0], 0)(part)
         read_chunks(res_ref, got_ref)
         acc_ref[...] = jnp.zeros_like(acc_ref)
 
     def step(b, k, refs):
-        f = made[k % 2]
-        fill = make(made[(k + 1) % 2], jnp.minimum(b + 1, LOCAL - 1))
+        f = made[k % count]
+        fill = make(made[(k + 1) % count], jnp.minimum(b + 1, LOCAL - 1))
         res = gather_windows(res_ref, windows(place_ref, b, 0))
         total = jnp.dot(res, refs[0][...], preferred_element_type=jnp.float32)
         x = updated(x_ref[b], total)
@@ -451,7 +449,7 @@
         out_shape=shape((count, 16, 128), jnp.int16),
         in_specs=[SM, VM],
         out_specs=VM,
-        scratch_shapes=[F_BUF, F_BUF, L_BUF, ACC_BUF],
+        scratch_shapes=[F_BUF] * 4 + [L_BUF, ACC_BUF],
         compiler_params=PARAMS,
     )(block_place, volume)
     def footprints(subset, start, *held):
@@ -482,13 +480,12 @@
         out_specs=(VM, VM),
         scratch_shapes=[
             F_RING,
-            F_BUF,
-            F_BUF,
             L_BUF,
             ACC_BUF,
             RES_BUF,
             pltpu.SemaphoreType.DMA((1, DEPTH)),
-        ],
+        ]
+        + [F_BUF] * 4,
         compiler_params=PARAMS,
     )(block_place, exchanged(rounded), volume, fa)
     fb, token = footprints(1, 0)

time: 139 us -> 134 us (0.964)
  Pallas kernels: 79.8 us -> 76.1 us
  waiting for transfers between devices: 25.9 us -> 24.4 us
    pallas_call x1, Pallas kernels: 24.7 us -> 20.8 us  [shards(): pl.pallas_call(middle_kernel, out_shape=(shape(volume.shape), shape((coun...]
    pallas_call x4, Pallas kernels: 24.9 us -> 26.4 us  [footprints(): pl.pallas_call(functools.partial(footprint_kernel, subset, start), out_sh...]
    all_to_all x4, waiting for transfers between devices: 25.9 us -> 24.4 us  [exchanged(): return lax.all_to_all(sent, axes, 0, 0, tiled=True)]
  transfers between devices with their start and end apart: 4 -> 4, of which waited for: 4 -> 4; matrix products, arithmetic and copies ran while one was open for 3% -> 3% of each run, Pallas kernels for 18% -> 20%
where the time goes in v4:
time: 134 us
  Pallas kernels  76.1 us (57%)
  starting transfers between devices  25.5 us (19%)
  waiting for transfers between devices  24.4 us (18%)
  local copies, waits for them, and re-layouts  6.45 us (5%)
    pallas_call x4, Pallas kernels, footprints(): pl.pallas_call(functools.partial(footprint_kernel, subset, start), out_sh...  26.4 us
    all_to_all x4, starting transfers between devices, exchanged(): return lax.all_to_all(sent, axes, 0, 0, tiled=True)  25.5 us
    all_to_all x4, waiting for transfers between devices, exchanged(): return lax.all_to_all(sent, axes, 0, 0, tiled=True)  24.4 us
    pallas_call x1, Pallas kernels, shards(): pl.pallas_call(middle_kernel, out_shape=(shape(volume.shape), shape((coun...  20.8 us
    pallas_call x1, Pallas kernels, shards(): pl.pallas_call(first_kernel, out_shape=shape((count, 16, 128), jnp.int16)...  15.7 us
    pallas_call x1, Pallas kernels, shards(): pl.pallas_call(last_kernel, out_shape=shape(volume.shape), in_specs=[SM,...  10.7 us
    unnamed x12, local copies, waits for them, and re-layouts  3.19 us
  transfers between devices with their start and end apart: 4, of which 4 were waited for; matrix products, arithmetic and copies ran while one was open for 3% of the time, Pallas kernels for 20%

profile of v4, /device:TPU:1, one launch (start us, length us, event | category | flops | bytes accessed | tf_op | source)
XLA Modules:
  0.0 133.8 jit_solution(7125486383136195128)
XLA Ops:
  0.6 1.2 copy-done
  1.9 0.7 copy-done.2
  2.5 15.7 %shard_map.59 = s16[128,16,128]{2,1,0:T(8,128)(2,1)} custom-call(s32[32]{0:T(128)S(1)} %copy-done.2, f32[32,8,1024]{2,1,0:T(8,128)S(1)} %copy-done), custom_call_target="tpu_custom_call" | custom-call | tf_op jit(solution)/shard_map/pallas_call | solution.py:447
  18.2 11.5 %all-to-all-start = ((s16[128,16,128]{2,1,0:T(8,128)(2,1)}), s16[128,16,128]{2,1,0:T(8,128)(2,1)S(1)}, u32[]{:S(2)}, u32[]{:S(2)}) async-start(s16[128,16,128]{2,1,0:T(8,128)(2,1)} %shard_map.59), calls=%async_computation | async-start | bytes 1048576 | tf_op jit(solution)/shard_map/all_to_all | solution.py:435
  29.7 0.8 fusion.9
  30.6 0.1 reshape.95
  30.8 0.1 reshape.96
  31.0 0.8 fusion.11
  31.9 0.1 reshape.98
  32.1 0.1 reshape.99
  32.2 0.1 fusion.3
  32.3 0.7 copy-done.3
  32.9 6.3 %shard_map.60 = (bf16[32,384,1024]{2,1,0:T(8,128)(2,1)}, f32[8,128]{1,0:T(8,128)S(1)}) custom-call(s32[32]{0:T(128)S(1)} %copy-done.3), custom_call_target="tpu_custom_call" | custom-call | bytes 12582912 | tf_op jit(solution)/shard_map/pallas_call | solution.py:456
  39.4 0.1 maximum_maximum_fusion.3
  39.5 4.1 %all-to-all-done.got_ref = s16[128,16,128]{2,1,0:T(8,128)(2,1)S(1)} async-done(((s16[128,16,128]{2,1,0:T(8,128)(2,1)}), s16[128,16,128]{2,1,0:T(8,128)(2,1)S(1)}, u32[]{:S(2)}, u32[]{:S(2)}) %all-to-all-start) | async-done | bytes 524320 | tf_op jit(solution)/shard_map/all_to_all | solution.py:435
  43.6 1.2 shard_map.61
  44.9 5.6 %all-to-all-start.1 = ((bf16[128,16,128]{2,1,0:T(8,128)(2,1)}), bf16[128,16,128]{2,1,0:T(8,128)(2,1)S(1)}, u32[]{:S(2)}, u32[]{:S(2)}) async-start(bf16[128,16,128]{2,1,0:T(8,128)(2,1)} %get-tuple-element.14), calls=%async_computation.1 | async-start | bytes 1048576 | tf_op jit(solution)/shard_map/all_to_all | solution.py:435
  50.5 0.6 copy-done.4
  51.2 6.9 %shard_map.62 = (bf16[32,384,1024]{2,1,0:T(8,128)(2,1)}, f32[8,128]{1,0:T(8,128)}) custom-call(s32[32]{0:T(128)S(1)} %copy-done.4, bf16[32,384,1024]{2,1,0:T(8,128)(2,1)} %get-tuple-element.15.refs_0_), custom_call_target="tpu_custom_call", output_to_operand_aliasing={{0}: (1, {})} | custom-call | bytes 12582912 | tf_op jit(solution)/shard_map/pallas_call | solution.py:456
  58.1 6.4 %all-to-all-done.1.got_ref = bf16[128,16,128]{2,1,0:T(8,128)(2,1)S(1)} async-done(((bf16[128,16,128]{2,1,0:T(8,128)(2,1)}), bf16[128,16,128]{2,1,0:T(8,128)(2,1)S(1)}, u32[]{:S(2)}, u32[]{:S(2)}) %all-to-all-start.1) | async-done | bytes 524320 | tf_op jit(solution)/shard_map/all_to_all | solution.py:435
  64.5 20.8 %shard_map.63 = (f32[32,8,1024]{2,1,0:T(8,128)S(1)}, s16[128,16,128]{2,1,0:T(8,128)(2,1)}) custom-call(s32[32]{0:T(128)S(1)} %copy-done.5, bf16[128,16,128]{2,1,0:T(8,128)(2,1)S(1)} %all-to-all-done.1.got_ref, f32[32,8,1024]{2,1,0:T(8,128)S(1)} %copy-done.1, bf16[32,384,1024]{2,1,0:T(8,128)(2,1)} %get-tuple-element.16.fa), custom_call_target="tpu_custom_call" | custom-call | tf_op jit(solution)/shard_map/pallas_call | solution.py:476
  85.2 4.2 %all-to-all-start.2 = ((s16[128,16,128]{2,1,0:T(8,128)(2,1)}), s16[128,16,128]{2,1,0:T(8,128)(2,1)S(1)}, u32[]{:S(2)}, u32[]{:S(2)}) async-start(s16[128,16,128]{2,1,0:T(8,128)(2,1)} %get-tuple-element.17), calls=%async_computation.2 | async-start | bytes 1048576 | tf_op jit(solution)/shard_map/all_to_all | solution.py:435
  89.4 6.3 %shard_map.64 = (bf16[32,384,1024]{2,1,0:T(8,128)(2,1)}, f32[8,128]{1,0:T(8,128)S(1)}) custom-call(s32[32]{0:T(128)S(1)} %copy-done.5), custom_call_target="tpu_custom_call" | custom-call | bytes 12582912 | tf_op jit(solution)/shard_map/pallas_call | solution.py:456
  95.7 7.7 %all-to-all-done.2.got_ref = s16[128,16,128]{2,1,0:T(8,128)(2,1)S(1)} async-done(((s16[128,16,128]{2,1,0:T(8,128)(2,1)}), s16[128,16,128]{2,1,0:T(8,128)(2,1)S(1)}, u32[]{:S(2)}, u32[]{:S(2)}) %all-to-all-start.2) | async-done | bytes 524320 | tf_op jit(solution)/shard_map/all_to_all | solution.py:435
  103.5 1.2 shard_map.65
  104.7 4.2 %all-to-all-start.3 = ((bf16[128,16,128]{2,1,0:T(8,128)(2,1)}), bf16[128,16,128]{2,1,0:T(8,128)(2,1)S(1)}, u32[]{:S(2)}, u32[]{:S(2)}) async-start(bf16[128,16,128]{2,1,0:T(8,128)(2,1)} %get-tuple-element.19), calls=%async_computation.3 | async-start | bytes 1048576 | tf_op jit(solution)/shard_map/all_to_all | solution.py:435
  108.9 6.9 %shard_map.66 = (bf16[32,384,1024]{2,1,0:T(8,128)(2,1)}, f32[8,128]{1,0:T(8,128)}) custom-call(s32[32]{0:T(128)S(1)} %copy-done.5, bf16[32,384,1024]{2,1,0:T(8,128)(2,1)} %get-tuple-element.21.refs_0_), custom_call_target="tpu_custom_call", output_to_operand_aliasing={{0}: (1, {})} | custom-call | bytes 12582912 | tf_op jit(solution)/shard_map/pallas_call | solution.py:456
  115.9 0.1 fusion
  116.0 0.1 copy.10
  116.1 0.7 reshape.97
  116.8 6.2 %all-to-all-done.3.got_ref = bf16[128,16,128]{2,1,0:T(8,128)(2,1)S(1)} async-done(((bf16[128,16,128]{2,1,0:T(8,128)(2,1)}), bf16[128,16,128]{2,1,0:T(8,128)(2,1)S(1)}, u32[]{:S(2)}, u32[]{:S(2)}) %all-to-all-start.3) | async-done | bytes 524320 | tf_op jit(solution)/shard_map/all_to_all | solution.py:435
  122.9 10.7 %shard_map.67 = f32[32,8,1024]{2,1,0:T(8,128)} custom-call(s32[32]{0:T(128)S(1)} %copy-done.5, bf16[128,16,128]{2,1,0:T(8,128)(2,1)S(1)} %all-to-all-done.3.got_ref, f32[32,8,1024]{2,1,0:T(8,128)S(1)} %get-tuple-element.20.x_ref, bf16[32,384,1024]{2,1,0:T(8,128)(2,1)} %get-tuple-element.22.fb), custom_call_target="tpu_custom_call" | custom-call | tf_op jit(solution)/shard_map/pallas_call | solution.py:494
  (29 shorter events, 0.7 us)
Async XLA Ops:
  0.6 1.2 copy-start
  1.9 0.7 copy-start.2
  2.5 61.9 %copy-start.1 = (f32[32,8,1024]{2,1,0:T(8,128)S(1)}, f32[32,8,1024]{2,1,0:T(8,128)}, u32[]{:S(2)}) copy-start(f32[32,8,1024]{2,1,0:T(8,128)} %x_ref.3) | copy-start | bytes 3145732
  2.5 61.9 %copy-start.5 = (s32[32]{0:T(128)S(1)}, s32[32]{0:T(128)}, u32[]{:S(2)}) copy-start(s32[32]{0:T(128)} %place_ref.13) | copy-start | bytes 388
  18.2 25.4 %all-to-all-start = ((s16[128,16,128]{2,1,0:T(8,128)(2,1)}), s16[128,16,128]{2,1,0:T(8,128)(2,1)S(1)}, u32[]{:S(2)}, u32[]{:S(2)}) async-start(s16[128,16,128]{2,1,0:T(8,128)(2,1)} %shard_map.59), calls=%async_computation | async-start | bytes 1048576 | tf_op jit(solution)/shard_map/all_to_all | solution.py:435
  32.3 0.7 copy-start.3
  44.9 19.6 %all-to-all-start.1 = ((bf16[128,16,128]{2,1,0:T(8,128)(2,1)}), bf16[128,16,128]{2,1,0:T(8,128)(2,1)S(1)}, u32[]{:S(2)}, u32[]{:S(2)}) async-start(bf16[128,16,128]{2,1,0:T(8,128)(2,1)} %get-tuple-element.14), calls=%async_computation.1 | async-start | bytes 1048576 | tf_op jit(solution)/shard_map/all_to_all | solution.py:435
  50.5 0.7 copy-start.4
  85.2 18.2 %all-to-all-start.2 = ((s16[128,16,128]{2,1,0:T(8,128)(2,1)}), s16[128,16,128]{2,1,0:T(8,128)(2,1)S(1)}, u32[]{:S(2)}, u32[]{:S(2)}) async-start(s16[128,16,128]{2,1,0:T(8,128)(2,1)} %get-tuple-element.17), calls=%async_computation.2 | async-start | bytes 1048576 | tf_op jit(solution)/shard_map/all_to_all | solution.py:435
  104.7 18.2 %all-to-all-start.3 = ((bf16[128,16,128]{2,1,0:T(8,128)(2,1)}), bf16[128,16,128]{2,1,0:T(8,128)(2,1)S(1)}, u32[]{:S(2)}, u32[]{:S(2)}) async-start(bf16[128,16,128]{2,1,0:T(8,128)(2,1)} %get-tuple-element.19), calls=%async_computation.3 | async-start | bytes 1048576 | tf_op jit(solution)/shard_map/all_to_all | solution.py:435

commit v5 on v4

--- a/solution.py
+++ b/solution.py
@@ -26,6 +26,7 @@
 CHUNKS = 16
 LOCAL = 32
 DEPTH = 12
+FIRST = 12
 MADE = 4
 TOGETHER = 4
 CODES = 32766.0
@@ -246,7 +247,7 @@
     return jnp.maximum(x + total[0:8] * (RELAX / total[8:9]), 0.0)
 
 
-def footprint_kernel(subset, start, place_ref, *refs):
+def footprint_kernel(subset, start, stop, place_ref, *refs):
     out_ref, token_ref, slots, l_ref, sems = refs[-5:]
     token_ref[...] = jnp.zeros_like(token_ref)
     fill_offsets(l_ref, subset)
@@ -267,9 +268,9 @@
             pltpu.make_async_copy(slots.at[k], out_ref.at[b], sems.at[k]).start()
         return carry
 
-    lax.fori_loop(0, LOCAL // 2 // MADE, some, 0)
+    lax.fori_loop(0, (stop - start) // MADE, some, 0)
     for k in range(MADE):
-        b = start + LOCAL // 2 - MADE + k
+        b = stop - MADE + k
         pltpu.make_async_copy(slots.at[k], out_ref.at[b], sems.at[k]).wait()
 
 
@@ -422,11 +423,12 @@
     own = ANG_SUB * NTILE // count
 
     def masks(subset):
-        rows = lax.dynamic_slice_in_dim(measured[subset], group * own, own, 0)
+        rows = lax.dynamic_slice(
+            measured, (subset, group * own, 0), (1, own, RAYS_TILE * NSL)
+        )
         rows = rows.reshape(own * RAYS_TILE, NSL).T
-        live = lax.dynamic_slice_in_dim(
-            live_rays[subset], (patch * lax.axis_size("group") + group) * own, own, 0
-        )
+        first = (patch * lax.axis_size("group") + group) * own
+        live = lax.dynamic_slice(live_rays, (subset, first), (1, own))[0]
         live = (jnp.arange(RAYS_TILE, dtype=jnp.int32)[None, :] < live[:, None]).astype(jnp.float32)
         live = jnp.broadcast_to(live.reshape(1, -1), (NSL, own * RAYS_TILE))
         return packed_rays(rows, odd), packed_rays(live, odd)
@@ -452,9 +454,9 @@
         scratch_shapes=[F_BUF] * 4 + [L_BUF, ACC_BUF],
         compiler_params=PARAMS,
     )(block_place, volume)
-    def footprints(subset, start, *held):
+    def footprints(subset, start, stop, *held):
         return pl.pallas_call(
-            functools.partial(footprint_kernel, subset, start),
+            functools.partial(footprint_kernel, subset, start, stop),
             out_shape=(shape((LOCAL, KALL, VOX), jnp.bfloat16), shape((8, 128))),
             in_specs=[SM] + [ANY] * len(held),
             out_specs=(ANY, VM),
@@ -466,13 +468,13 @@
             input_output_aliases={1: 0} if held else {},
             compiler_params=PARAMS,
             cost_estimate=pl.CostEstimate(
-                flops=0, bytes_accessed=LOCAL * KALL * VOX, transcendentals=0
+                flops=0, bytes_accessed=(stop - start) * KALL * VOX * 2, transcendentals=0
             ),
         )(block_place, *held)
 
-    fa, token = footprints(0, 0)
+    fa, token = footprints(0, 0, FIRST)
     _, rounded = residual(sent, 0, token)
-    fa, _ = footprints(0, LOCAL // 2, fa)
+    fa, _ = footprints(0, FIRST, LOCAL, fa)
     estimate, sent = pl.pallas_call(
         middle_kernel,
         out_shape=(shape(volume.shape), shape((count, 16, 128), jnp.int16)),
@@ -488,9 +490,9 @@
         + [F_BUF] * 4,
         compiler_params=PARAMS,
     )(block_place, exchanged(rounded), volume, fa)
-    fb, token = footprints(1, 0)
+    fb, token = footprints(1, 0, LOCAL // 2)
     last, rounded = residual(sent, 1, token)
-    fb, _ = footprints(1, LOCAL // 2, fb)
+    fb, _ = footprints(1, LOCAL // 2, LOCAL, fb)
     final = pl.pallas_call(
         last_kernel,
         out_shape=shape(volume.shape),

time: 134 us -> 133 us (level)
    slice x2 -> x0, local copies, waits for them, and re-layouts: 1.6 us -> none  [the longest x1 0.83 us: masks(): rows = lax.dynamic_slice_in_dim(measured[subset], group * own, own, 0)]
where the time goes in v5:
time: 133 us
  Pallas kernels  76 us (57%)
  starting transfers between devices  24.5 us (18%)
  waiting for transfers between devices  24.5 us (18%)
  local copies, waits for them, and re-layouts  6.25 us (5%)
    pallas_call x4, Pallas kernels, footprints(): pl.pallas_call(functools.partial(footprint_kernel, subset, start, stop),...  26.4 us
    all_to_all x4, starting transfers between devices, exchanged(): return lax.all_to_all(sent, axes, 0, 0, tiled=True)  24.5 us
    all_to_all x4, waiting for transfers between devices, exchanged(): return lax.all_to_all(sent, axes, 0, 0, tiled=True)  24.5 us
    pallas_call x1, Pallas kernels, shards(): pl.pallas_call(middle_kernel, out_shape=(shape(volume.shape), shape((coun...  20.8 us
    pallas_call x1, Pallas kernels, shards(): pl.pallas_call(first_kernel, out_shape=shape((count, 16, 128), jnp.int16)...  15.7 us
    pallas_call x1, Pallas kernels, shards(): pl.pallas_call(last_kernel, out_shape=shape(volume.shape), in_specs=[SM,...  10.7 us
    unnamed x12, local copies, waits for them, and re-layouts  3.19 us
  transfers between devices with their start and end apart: 4, of which 4 were waited for; matrix products, arithmetic and copies ran while one was open for 3% of the time, Pallas kernels for 20%

profile of v5, /device:TPU:1, one launch (start us, length us, event | category | flops | bytes accessed | tf_op | source)
XLA Modules:
  0.0 132.7 jit_solution(6408769120075759686)
XLA Ops:
  0.6 1.2 copy-done
  1.9 0.7 copy-done.2
  2.5 15.7 %shard_map.59 = s16[128,16,128]{2,1,0:T(8,128)(2,1)} custom-call(s32[32]{0:T(128)S(1)} %copy-done.2, f32[32,8,1024]{2,1,0:T(8,128)S(1)} %copy-done), custom_call_target="tpu_custom_call" | custom-call | tf_op jit(solution)/shard_map/pallas_call | solution.py:449
  18.2 11.5 %all-to-all-start = ((s16[128,16,128]{2,1,0:T(8,128)(2,1)}), s16[128,16,128]{2,1,0:T(8,128)(2,1)S(1)}, u32[]{:S(2)}, u32[]{:S(2)}) async-start(s16[128,16,128]{2,1,0:T(8,128)(2,1)} %shard_map.59), calls=%async_computation | async-start | bytes 1048576 | tf_op jit(solution)/shard_map/all_to_all | solution.py:437
  29.7 0.7 constant_dynamic-slice_fusion
  30.5 0.1 reshape.87
  30.6 0.1 reshape.88
  30.9 0.8 dynamic-slice_bitcast_fusion
  31.8 0.1 reshape.90
  31.9 0.1 reshape.91
  32.0 0.1 fusion.4
  32.1 0.7 copy-done.3
  32.8 5.2 %shard_map.60 = (bf16[32,384,1024]{2,1,0:T(8,128)(2,1)}, f32[8,128]{1,0:T(8,128)S(1)}) custom-call(s32[32]{0:T(128)S(1)} %copy-done.3), custom_call_target="tpu_custom_call" | custom-call | bytes 9437184 | tf_op jit(solution)/shard_map/pallas_call | solution.py:458
  38.1 0.1 maximum_maximum_fusion.3
  38.2 5.5 %all-to-all-done.got_ref = s16[128,16,128]{2,1,0:T(8,128)(2,1)S(1)} async-done(((s16[128,16,128]{2,1,0:T(8,128)(2,1)}), s16[128,16,128]{2,1,0:T(8,128)(2,1)S(1)}, u32[]{:S(2)}, u32[]{:S(2)}) %all-to-all-start) | async-done | bytes 524320 | tf_op jit(solution)/shard_map/all_to_all | solution.py:437
  43.6 1.2 shard_map.61
  44.9 4.3 %all-to-all-start.1 = ((bf16[128,16,128]{2,1,0:T(8,128)(2,1)}), bf16[128,16,128]{2,1,0:T(8,128)(2,1)S(1)}, u32[]{:S(2)}, u32[]{:S(2)}) async-start(bf16[128,16,128]{2,1,0:T(8,128)(2,1)} %get-tuple-element.14), calls=%async_computation.1 | async-start | bytes 1048576 | tf_op jit(solution)/shard_map/all_to_all | solution.py:437
  49.2 0.6 copy-done.4
  49.8 8.0 %shard_map.62 = (bf16[32,384,1024]{2,1,0:T(8,128)(2,1)}, f32[8,128]{1,0:T(8,128)}) custom-call(s32[32]{0:T(128)S(1)} %copy-done.4, bf16[32,384,1024]{2,1,0:T(8,128)(2,1)} %get-tuple-element.15.refs_0_), custom_call_target="tpu_custom_call", output_to_operand_aliasing={{0}: (1, {})} | custom-call | bytes 15728640 | tf_op jit(solution)/shard_map/pallas_call | solution.py:458
  57.8 5.3 %all-to-all-done.1.got_ref = bf16[128,16,128]{2,1,0:T(8,128)(2,1)S(1)} async-done(((bf16[128,16,128]{2,1,0:T(8,128)(2,1)}), bf16[128,16,128]{2,1,0:T(8,128)(2,1)S(1)}, u32[]{:S(2)}, u32[]{:S(2)}) %all-to-all-start.1) | async-done | bytes 524320 | tf_op jit(solution)/shard_map/all_to_all | solution.py:437
  63.1 20.8 %shard_map.63 = (f32[32,8,1024]{2,1,0:T(8,128)S(1)}, s16[128,16,128]{2,1,0:T(8,128)(2,1)}) custom-call(s32[32]{0:T(128)S(1)} %copy-done.5, bf16[128,16,128]{2,1,0:T(8,128)(2,1)S(1)} %all-to-all-done.1.got_ref, f32[32,8,1024]{2,1,0:T(8,128)S(1)} %copy-done.1, bf16[32,384,1024]{2,1,0:T(8,128)(2,1)} %get-tuple-element.16.fa), custom_call_target="tpu_custom_call" | custom-call | tf_op jit(solution)/shard_map/pallas_call | solution.py:478
  83.9 4.6 %all-to-all-start.2 = ((s16[128,16,128]{2,1,0:T(8,128)(2,1)}), s16[128,16,128]{2,1,0:T(8,128)(2,1)S(1)}, u32[]{:S(2)}, u32[]{:S(2)}) async-start(s16[128,16,128]{2,1,0:T(8,128)(2,1)} %get-tuple-element.17), calls=%async_computation.2 | async-start | bytes 1048576 | tf_op jit(solution)/shard_map/all_to_all | solution.py:437
  88.5 6.3 %shard_map.64 = (bf16[32,384,1024]{2,1,0:T(8,128)(2,1)}, f32[8,128]{1,0:T(8,128)S(1)}) custom-call(s32[32]{0:T(128)S(1)} %copy-done.5), custom_call_target="tpu_custom_call" | custom-call | bytes 12582912 | tf_op jit(solution)/shard_map/pallas_call | solution.py:458
  94.8 7.6 %all-to-all-done.2.got_ref = s16[128,16,128]{2,1,0:T(8,128)(2,1)S(1)} async-done(((s16[128,16,128]{2,1,0:T(8,128)(2,1)}), s16[128,16,128]{2,1,0:T(8,128)(2,1)S(1)}, u32[]{:S(2)}, u32[]{:S(2)}) %all-to-all-start.2) | async-done | bytes 524320 | tf_op jit(solution)/shard_map/all_to_all | solution.py:437
  102.4 1.2 shard_map.65
  103.6 4.2 %all-to-all-start.3 = ((bf16[128,16,128]{2,1,0:T(8,128)(2,1)}), bf16[128,16,128]{2,1,0:T(8,128)(2,1)S(1)}, u32[]{:S(2)}, u32[]{:S(2)}) async-start(bf16[128,16,128]{2,1,0:T(8,128)(2,1)} %get-tuple-element.19), calls=%async_computation.3 | async-start | bytes 1048576 | tf_op jit(solution)/shard_map/all_to_all | solution.py:437
  107.8 6.9 %shard_map.66 = (bf16[32,384,1024]{2,1,0:T(8,128)(2,1)}, f32[8,128]{1,0:T(8,128)}) custom-call(s32[32]{0:T(128)S(1)} %copy-done.5, bf16[32,384,1024]{2,1,0:T(8,128)(2,1)} %get-tuple-element.21.refs_0_), custom_call_target="tpu_custom_call", output_to_operand_aliasing={{0}: (1, {})} | custom-call | bytes 12582912 | tf_op jit(solution)/shard_map/pallas_call | solution.py:458
  114.8 0.1 fusion
  114.9 0.1 copy.10
  115.0 0.7 reshape.89
  115.7 6.2 %all-to-all-done.3.got_ref = bf16[128,16,128]{2,1,0:T(8,128)(2,1)S(1)} async-done(((bf16[128,16,128]{2,1,0:T(8,128)(2,1)}), bf16[128,16,128]{2,1,0:T(8,128)(2,1)S(1)}, u32[]{:S(2)}, u32[]{:S(2)}) %all-to-all-start.3) | async-done | bytes 524320 | tf_op jit(solution)/shard_map/all_to_all | solution.py:437
  121.8 10.7 %shard_map.67 = f32[32,8,1024]{2,1,0:T(8,128)} custom-call(s32[32]{0:T(128)S(1)} %copy-done.5, bf16[128,16,128]{2,1,0:T(8,128)(2,1)S(1)} %all-to-all-done.3.got_ref, f32[32,8,1024]{2,1,0:T(8,128)S(1)} %get-tuple-element.20.x_ref, bf16[32,384,1024]{2,1,0:T(8,128)(2,1)} %get-tuple-element.22.fb), custom_call_target="tpu_custom_call" | custom-call | tf_op jit(solution)/shard_map/pallas_call | solution.py:496
  (25 shorter events, 0.5 us)
Async XLA Ops:
  0.6 1.2 copy-start
  1.9 0.7 copy-start.2
  2.5 60.6 %copy-start.1 = (f32[32,8,1024]{2,1,0:T(8,128)S(1)}, f32[32,8,1024]{2,1,0:T(8,128)}, u32[]{:S(2)}) copy-start(f32[32,8,1024]{2,1,0:T(8,128)} %x_ref.3) | copy-start | bytes 3145732
  2.5 60.6 %copy-start.5 = (s32[32]{0:T(128)S(1)}, s32[32]{0:T(128)}, u32[]{:S(2)}) copy-start(s32[32]{0:T(128)} %place_ref.13) | copy-start | bytes 388
  18.2 25.4 %all-to-all-start = ((s16[128,16,128]{2,1,0:T(8,128)(2,1)}), s16[128,16,128]{2,1,0:T(8,128)(2,1)S(1)}, u32[]{:S(2)}, u32[]{:S(2)}) async-start(s16[128,16,128]{2,1,0:T(8,128)(2,1)} %shard_map.59), calls=%async_computation | async-start | bytes 1048576 | tf_op jit(solution)/shard_map/all_to_all | solution.py:437
  32.1 0.7 copy-start.3
  44.9 18.2 %all-to-all-start.1 = ((bf16[128,16,128]{2,1,0:T(8,128)(2,1)}), bf16[128,16,128]{2,1,0:T(8,128)(2,1)S(1)}, u32[]{:S(2)}, u32[]{:S(2)}) async-start(bf16[128,16,128]{2,1,0:T(8,128)(2,1)} %get-tuple-element.14), calls=%async_computation.1 | async-start | bytes 1048576 | tf_op jit(solution)/shard_map/all_to_all | solution.py:437
  49.2 0.7 copy-start.4
  83.9 18.5 %all-to-all-start.2 = ((s16[128,16,128]{2,1,0:T(8,128)(2,1)}), s16[128,16,128]{2,1,0:T(8,128)(2,1)S(1)}, u32[]{:S(2)}, u32[]{:S(2)}) async-start(s16[128,16,128]{2,1,0:T(8,128)(2,1)} %get-tuple-element.17), calls=%async_computation.2 | async-start | bytes 1048576 | tf_op jit(solution)/shard_map/all_to_all | solution.py:437
  103.6 18.2 %all-to-all-start.3 = ((bf16[128,16,128]{2,1,0:T(8,128)(2,1)}), bf16[128,16,128]{2,1,0:T(8,128)(2,1)S(1)}, u32[]{:S(2)}, u32[]{:S(2)}) async-start(bf16[128,16,128]{2,1,0:T(8,128)(2,1)} %get-tuple-element.19), calls=%async_computation.3 | async-start | bytes 1048576 | tf_op jit(solution)/shard_map/all_to_all | solution.py:437

commit v6 on v5

--- a/solution.py
+++ b/solution.py
@@ -369,7 +369,7 @@
         return tuple(out)
 
     zero = jnp.zeros((16, 128), jnp.float32)
-    parts = lax.fori_loop(0, count // 4, add, (zero,) * 4, unroll=4)
+    parts = lax.fori_loop(0, count // 4, add, (zero,) * 4, unroll=8)
     total = (parts[0] + parts[1]) + (parts[2] + parts[3])
     sums = jnp.where(row < 8, total[12:13], total[13:14])
     differ = (meas_ref[...] - total / jnp.maximum(sums, 1.0)) * live_ref[...]
@@ -451,7 +451,7 @@
         out_shape=shape((count, 16, 128), jnp.int16),
         in_specs=[SM, VM],
         out_specs=VM,
-        scratch_shapes=[F_BUF] * 4 + [L_BUF, ACC_BUF],
+        scratch_shapes=[F_BUF] * 8 + [L_BUF, ACC_BUF],
         compiler_params=PARAMS,
     )(block_place, volume)
     def footprints(subset, start, stop, *held):

time: 133 us -> 133 us (level)
  no operation moved by 1% of the time
where the time goes in v6:
time: 133 us; the launch traced here: 132 us
  Pallas kernels  75.6 us (57%)
  starting transfers between devices  24.5 us (18%)
  waiting for transfers between devices  24.5 us (18%)
  local copies, waits for them, and re-layouts  6.25 us (5%)
    pallas_call x4, Pallas kernels, footprints(): pl.pallas_call(functools.partial(footprint_kernel, subset, start, stop),...  26.4 us
    all_to_all x4, starting transfers between devices, exchanged(): return lax.all_to_all(sent, axes, 0, 0, tiled=True)  24.5 us
    all_to_all x4, waiting for transfers between devices, exchanged(): return lax.all_to_all(sent, axes, 0, 0, tiled=True)  24.5 us
    pallas_call x1, Pallas kernels, shards(): pl.pallas_call(middle_kernel, out_shape=(shape(volume.shape), shape((coun...  20.8 us
    pallas_call x1, Pallas kernels, shards(): pl.pallas_call(first_kernel, out_shape=shape((count, 16, 128), jnp.int16)...  15.4 us
    pallas_call x1, Pallas kernels, shards(): pl.pallas_call(last_kernel, out_shape=shape(volume.shape), in_specs=[SM,...  10.7 us
    unnamed x12, local copies, waits for them, and re-layouts  3.19 us
  transfers between devices with their start and end apart: 4, of which 4 were waited for; matrix products, arithmetic and copies ran while one was open for 3% of the time, Pallas kernels for 20%

profile of v6, /device:TPU:1, one launch (start us, length us, event | category | flops | bytes accessed | tf_op | source)
XLA Modules:
  0.0 132.3 jit_solution(2986184630256153106)
XLA Ops:
  0.6 1.2 copy-done
  1.9 0.7 copy-done.2
  2.5 15.4 %shard_map.59 = s16[128,16,128]{2,1,0:T(8,128)(2,1)} custom-call(s32[32]{0:T(128)S(1)} %copy-done.2, f32[32,8,1024]{2,1,0:T(8,128)S(1)} %copy-done), custom_call_target="tpu_custom_call" | custom-call | tf_op jit(solution)/shard_map/pallas_call | solution.py:449
  17.9 11.5 %all-to-all-start = ((s16[128,16,128]{2,1,0:T(8,128)(2,1)}), s16[128,16,128]{2,1,0:T(8,128)(2,1)S(1)}, u32[]{:S(2)}, u32[]{:S(2)}) async-start(s16[128,16,128]{2,1,0:T(8,128)(2,1)} %shard_map.59), calls=%async_computation | async-start | bytes 1048576 | tf_op jit(solution)/shard_map/all_to_all | solution.py:437
  29.4 0.7 constant_dynamic-slice_fusion
  30.1 0.1 reshape.87
  30.3 0.1 reshape.88
  30.5 0.8 dynamic-slice_bitcast_fusion
  31.4 0.1 reshape.90
  31.6 0.1 reshape.91
  31.7 0.1 fusion.4
  31.7 0.7 copy-done.3
  32.4 5.2 %shard_map.60 = (bf16[32,384,1024]{2,1,0:T(8,128)(2,1)}, f32[8,128]{1,0:T(8,128)S(1)}) custom-call(s32[32]{0:T(128)S(1)} %copy-done.3), custom_call_target="tpu_custom_call" | custom-call | bytes 9437184 | tf_op jit(solution)/shard_map/pallas_call | solution.py:458
  37.7 0.1 maximum_maximum_fusion.3
  37.8 5.5 %all-to-all-done.got_ref = s16[128,16,128]{2,1,0:T(8,128)(2,1)S(1)} async-done(((s16[128,16,128]{2,1,0:T(8,128)(2,1)}), s16[128,16,128]{2,1,0:T(8,128)(2,1)S(1)}, u32[]{:S(2)}, u32[]{:S(2)}) %all-to-all-start) | async-done | bytes 524320 | tf_op jit(solution)/shard_map/all_to_all | solution.py:437
  43.3 1.2 shard_map.61
  44.5 4.3 %all-to-all-start.1 = ((bf16[128,16,128]{2,1,0:T(8,128)(2,1)}), bf16[128,16,128]{2,1,0:T(8,128)(2,1)S(1)}, u32[]{:S(2)}, u32[]{:S(2)}) async-start(bf16[128,16,128]{2,1,0:T(8,128)(2,1)} %get-tuple-element.14), calls=%async_computation.1 | async-start | bytes 1048576 | tf_op jit(solution)/shard_map/all_to_all | solution.py:437
  48.8 0.6 copy-done.4
  49.5 8.0 %shard_map.62 = (bf16[32,384,1024]{2,1,0:T(8,128)(2,1)}, f32[8,128]{1,0:T(8,128)}) custom-call(s32[32]{0:T(128)S(1)} %copy-done.4, bf16[32,384,1024]{2,1,0:T(8,128)(2,1)} %get-tuple-element.15.refs_0_), custom_call_target="tpu_custom_call", output_to_operand_aliasing={{0}: (1, {})} | custom-call | bytes 15728640 | tf_op jit(solution)/shard_map/pallas_call | solution.py:458
  57.5 5.3 %all-to-all-done.1.got_ref = bf16[128,16,128]{2,1,0:T(8,128)(2,1)S(1)} async-done(((bf16[128,16,128]{2,1,0:T(8,128)(2,1)}), bf16[128,16,128]{2,1,0:T(8,128)(2,1)S(1)}, u32[]{:S(2)}, u32[]{:S(2)}) %all-to-all-start.1) | async-done | bytes 524320 | tf_op jit(solution)/shard_map/all_to_all | solution.py:437
  62.8 20.8 %shard_map.63 = (f32[32,8,1024]{2,1,0:T(8,128)S(1)}, s16[128,16,128]{2,1,0:T(8,128)(2,1)}) custom-call(s32[32]{0:T(128)S(1)} %copy-done.5, bf16[128,16,128]{2,1,0:T(8,128)(2,1)S(1)} %all-to-all-done.1.got_ref, f32[32,8,1024]{2,1,0:T(8,128)S(1)} %copy-done.1, bf16[32,384,1024]{2,1,0:T(8,128)(2,1)} %get-tuple-element.16.fa), custom_call_target="tpu_custom_call" | custom-call | tf_op jit(solution)/shard_map/pallas_call | solution.py:478
  83.5 4.6 %all-to-all-start.2 = ((s16[128,16,128]{2,1,0:T(8,128)(2,1)}), s16[128,16,128]{2,1,0:T(8,128)(2,1)S(1)}, u32[]{:S(2)}, u32[]{:S(2)}) async-start(s16[128,16,128]{2,1,0:T(8,128)(2,1)} %get-tuple-element.17), calls=%async_computation.2 | async-start | bytes 1048576 | tf_op jit(solution)/shard_map/all_to_all | solution.py:437
  88.1 6.3 %shard_map.64 = (bf16[32,384,1024]{2,1,0:T(8,128)(2,1)}, f32[8,128]{1,0:T(8,128)S(1)}) custom-call(s32[32]{0:T(128)S(1)} %copy-done.5), custom_call_target="tpu_custom_call" | custom-call | bytes 12582912 | tf_op jit(solution)/shard_map/pallas_call | solution.py:458
  94.4 7.6 %all-to-all-done.2.got_ref = s16[128,16,128]{2,1,0:T(8,128)(2,1)S(1)} async-done(((s16[128,16,128]{2,1,0:T(8,128)(2,1)}), s16[128,16,128]{2,1,0:T(8,128)(2,1)S(1)}, u32[]{:S(2)}, u32[]{:S(2)}) %all-to-all-start.2) | async-done | bytes 524320 | tf_op jit(solution)/shard_map/all_to_all | solution.py:437
  102.0 1.2 shard_map.65
  103.2 4.2 %all-to-all-start.3 = ((bf16[128,16,128]{2,1,0:T(8,128)(2,1)}), bf16[128,16,128]{2,1,0:T(8,128)(2,1)S(1)}, u32[]{:S(2)}, u32[]{:S(2)}) async-start(bf16[128,16,128]{2,1,0:T(8,128)(2,1)} %get-tuple-element.19), calls=%async_computation.3 | async-start | bytes 1048576 | tf_op jit(solution)/shard_map/all_to_all | solution.py:437
  107.4 6.9 %shard_map.66 = (bf16[32,384,1024]{2,1,0:T(8,128)(2,1)}, f32[8,128]{1,0:T(8,128)}) custom-call(s32[32]{0:T(128)S(1)} %copy-done.5, bf16[32,384,1024]{2,1,0:T(8,128)(2,1)} %get-tuple-element.21.refs_0_), custom_call_target="tpu_custom_call", output_to_operand_aliasing={{0}: (1, {})} | custom-call | bytes 12582912 | tf_op jit(solution)/shard_map/pallas_call | solution.py:458
  114.4 0.1 fusion
  114.5 0.1 copy.10
  114.6 0.7 reshape.89
  115.3 6.2 %all-to-all-done.3.got_ref = bf16[128,16,128]{2,1,0:T(8,128)(2,1)S(1)} async-done(((bf16[128,16,128]{2,1,0:T(8,128)(2,1)}), bf16[128,16,128]{2,1,0:T(8,128)(2,1)S(1)}, u32[]{:S(2)}, u32[]{:S(2)}) %all-to-all-start.3) | async-done | bytes 524320 | tf_op jit(solution)/shard_map/all_to_all | solution.py:437
  121.5 10.7 %shard_map.67 = f32[32,8,1024]{2,1,0:T(8,128)} custom-call(s32[32]{0:T(128)S(1)} %copy-done.5, bf16[128,16,128]{2,1,0:T(8,128)(2,1)S(1)} %all-to-all-done.3.got_ref, f32[32,8,1024]{2,1,0:T(8,128)S(1)} %get-tuple-element.20.x_ref, bf16[32,384,1024]{2,1,0:T(8,128)(2,1)} %get-tuple-element.22.fb), custom_call_target="tpu_custom_call" | custom-call | tf_op jit(solution)/shard_map/pallas_call | solution.py:496
  (25 shorter events, 0.5 us)
Async XLA Ops:
  0.6 1.2 copy-start
  1.9 0.7 copy-start.2
  2.5 60.2 %copy-start.1 = (f32[32,8,1024]{2,1,0:T(8,128)S(1)}, f32[32,8,1024]{2,1,0:T(8,128)}, u32[]{:S(2)}) copy-start(f32[32,8,1024]{2,1,0:T(8,128)} %x_ref.3) | copy-start | bytes 3145732
  2.5 60.2 %copy-start.5 = (s32[32]{0:T(128)S(1)}, s32[32]{0:T(128)}, u32[]{:S(2)}) copy-start(s32[32]{0:T(128)} %place_ref.13) | copy-start | bytes 388
  17.9 25.4 %all-to-all-start = ((s16[128,16,128]{2,1,0:T(8,128)(2,1)}), s16[128,16,128]{2,1,0:T(8,128)(2,1)S(1)}, u32[]{:S(2)}, u32[]{:S(2)}) async-start(s16[128,16,128]{2,1,0:T(8,128)(2,1)} %shard_map.59), calls=%async_computation | async-start | bytes 1048576 | tf_op jit(solution)/shard_map/all_to_all | solution.py:437
  31.7 0.7 copy-start.3
  44.5 18.2 %all-to-all-start.1 = ((bf16[128,16,128]{2,1,0:T(8,128)(2,1)}), bf16[128,16,128]{2,1,0:T(8,128)(2,1)S(1)}, u32[]{:S(2)}, u32[]{:S(2)}) async-start(bf16[128,16,128]{2,1,0:T(8,128)(2,1)} %get-tuple-element.14), calls=%async_computation.1 | async-start | bytes 1048576 | tf_op jit(solution)/shard_map/all_to_all | solution.py:437
  48.8 0.7 copy-start.4
  83.5 18.5 %all-to-all-start.2 = ((s16[128,16,128]{2,1,0:T(8,128)(2,1)}), s16[128,16,128]{2,1,0:T(8,128)(2,1)S(1)}, u32[]{:S(2)}, u32[]{:S(2)}) async-start(s16[128,16,128]{2,1,0:T(8,128)(2,1)} %get-tuple-element.17), calls=%async_computation.2 | async-start | bytes 1048576 | tf_op jit(solution)/shard_map/all_to_all | solution.py:437
  103.2 18.2 %all-to-all-start.3 = ((bf16[128,16,128]{2,1,0:T(8,128)(2,1)}), bf16[128,16,128]{2,1,0:T(8,128)(2,1)S(1)}, u32[]{:S(2)}, u32[]{:S(2)}) async-start(bf16[128,16,128]{2,1,0:T(8,128)(2,1)} %get-tuple-element.19), calls=%async_computation.3 | async-start | bytes 1048576 | tf_op jit(solution)/shard_map/all_to_all | solution.py:437
